TPU v7x, 256 devices: a whole 4x4x8 slice. The times are simulated.
256 devices in a mesh: row: 4 (over x), col: 64 (over y, z, core).
Axes of the slice: x: 4, y: 4, z: 8, core: 2. Of those that a mesh axis runs over, the one named last changes fastest.
Arguments:
- source: bfloat16 [32768, 128], P(('row', 'col')), may hold values from -6 to 6
- target: bfloat16 [32768, 128], P('col'), may hold values from -6 to 6
- potential: float32 [32768], P('col'), may hold values from -0.3 to 0.3
Outputs:
- source_potential: float32 [32768], P(('row', 'col'))
- target_potential: float32 [32768], P('col')
- mapped: bfloat16 [32768, 128], P(('row', 'col'))
All inputs are finite; a program needn't handle non-finite values.
Results may differ from a plain program's by a relative error of at most 0.008.
Values may be sent and summed in bfloat16 or wider, within the bound.
A program may use at most 64 MiB of HBM per device.

v0:
```python
import math

import jax
import jax.numpy as jnp
from jax import lax
from jax.sharding import PartitionSpec as P

D = 128


epsilon = 0.02


def cost_tile(block_rows, target, target_sq):
    row_sq = jnp.sum(jnp.square(block_rows.astype(jnp.float32)), axis=1)
    inner = lax.dot_general(
        block_rows, target, (((1,), (1,)), ((), ())), preferred_element_type=jnp.float32
    )
    return (row_sq[:, None] + target_sq[None, :] - 2.0 * inner) / (2.0 * D)


def local(source, target, potential):
    own_rows = source.shape[0]
    col_count = lax.axis_size("col")
    row_count = lax.axis_size("row")
    gathered = lax.all_gather(source, "col", axis=0, tiled=True)
    block_total = gathered.shape[0]
    all_sources = block_total * row_count
    all_targets = target.shape[0] * col_count
    block_size = math.gcd(block_total, 512)
    target_sq = jnp.sum(jnp.square(target.astype(jnp.float32)), axis=1)
    blocks = gathered.reshape(block_total // block_size, block_size, gathered.shape[1])

    def row_pass(block_rows):
        scores = (potential[None, :] - cost_tile(block_rows, target, target_sq)) / epsilon
        peak = jnp.max(scores, axis=1)
        return (peak, jnp.sum(jnp.exp(scores - peak[:, None]), axis=1))

    row_peak, row_sum = lax.map(row_pass, blocks)
    row_peak = row_peak.reshape(block_total)
    row_sum = row_sum.reshape(block_total)
    top_peak = lax.pmax(row_peak.astype(jnp.bfloat16), "col").astype(row_peak.dtype)
    top_sum = lax.psum(row_sum * jnp.exp(row_peak - top_peak), "col")
    f_whole = -epsilon * (top_peak + jnp.log(top_sum)) - epsilon * math.log(all_sources)
    f_blocks = f_whole.reshape(block_total // block_size, block_size)

    def column_step(carry, items):
        peak, total = carry
        block_rows, f_block = items
        scores = (f_block[:, None] - cost_tile(block_rows, target, target_sq)) / epsilon
        new_peak = jnp.maximum(peak, jnp.max(scores, axis=0))
        total = total * jnp.exp(peak - new_peak) + jnp.sum(
            jnp.exp(scores - new_peak[None, :]), axis=0
        )
        return ((new_peak, total), None)

    start = (
        jnp.full(potential.shape, -jnp.inf, jnp.float32),
        jnp.zeros(potential.shape, jnp.float32),
    )
    (col_peak, col_sum), unused = lax.scan(column_step, start, (blocks, f_blocks))
    high_peak = lax.pmax(col_peak, "row")
    high_sum = lax.psum(col_sum * jnp.exp(col_peak - high_peak), "row")
    target_potential = -epsilon * (high_peak + jnp.log(high_sum)) - epsilon * math.log(all_targets)

    def bary_pass(items):
        block_rows, f_block = items
        plan = jnp.exp(
            (
                f_block[:, None]
                + target_potential[None, :]
                - cost_tile(block_rows, target, target_sq)
            )
            / epsilon
        )
        weight = jnp.sum(plan, axis=1)
        weighted = jnp.dot(plan.astype(jnp.bfloat16), target, preferred_element_type=jnp.float32)
        return (weighted, weight)

    numerator, denominator = lax.map(bary_pass, (blocks, f_blocks))
    numerator = numerator.reshape(block_total, target.shape[1])
    denominator = denominator.reshape(block_total)
    offset = lax.axis_index("col") * own_rows
    full_num, full_den = lax.psum((numerator, denominator), "col")
    own_num = lax.dynamic_slice_in_dim(full_num, offset, own_rows, 0)
    own_den = lax.dynamic_slice_in_dim(full_den, offset, own_rows, 0)
    mapped = (own_num / own_den[:, None]).astype(jnp.bfloat16)
    source_potential = lax.dynamic_slice_in_dim(f_whole, offset, own_rows, 0)
    return (source_potential, target_potential, mapped)


def solution(mesh):
    placed = (P(("row", "col"), None), P("col", None), P("col"))
    return jax.shard_map(
        local,
        mesh=mesh,
        in_specs=placed,
        out_specs=(P(("row", "col")), P("col"), P(("row", "col"), None)),
        check_vma=False,
    )
```

profile of v0, /device:TPU:1, one launch (start us, length us, event | category | flops | bytes accessed | tf_op | source)
XLA Modules:
  0.0 1004.7 jit_solution(15389082024174366851)
XLA Ops:
  9.0 83.3 %all-gather.2.cloned.1.call-done = bf16[8192,128]{1,0:T(8,128)(2,1)} async-done(((bf16[128,128]{1,0:T(8,128)(2,1)}), bf16[8192,128]{1,0:T(8,128)(2,1)}) %all-gather.2.cloned.1.call-update) | async-done | bytes 2097168 | tf_op jit(solution)/shard_map/all_gather | solution.py:26
  92.4 44.7 %while.37 = (s32[]{:T(128)}, f32[16,512]{1,0:T(8,128)S(1)}, f32[16,512]{1,0:T(8,128)S(1)}, f32[512]{0:T(512)}, bf16[16,512,128]{2,1,0:T(8,128)(2,1)}, /*index=5*...) while((s32[]{:T(128)}, f32[16,512]{1,0:T(8,128)S(1)}, f32[16,512]{1,0:T(8,128)S(1)}, ...), condition=%wide.region_5.6_spmd, body=%wide.region_1.5_spmd.sunk | while | flops 69663232 | bytes 2513013 | solution.py:39
  93.4 1.4 fusion.48
  96.2 1.4 fusion.48
  99.0 1.4 fusion.48
  101.8 1.4 fusion.48
  104.6 1.4 fusion.48
  107.4 1.4 fusion.48
  110.2 1.4 fusion.48
  113.0 1.4 fusion.48
  115.8 1.4 fusion.48
  118.5 1.4 fusion.48
  121.3 1.4 fusion.48
  124.1 1.4 fusion.48
  126.9 1.4 fusion.48
  129.7 1.4 fusion.48
  132.5 1.4 fusion.48
  135.3 1.4 fusion.48
  137.1 243.4 %pmax.14 = bf16[8192]{0:T(1024)(128)(2,1)S(1)} all-reduce(bf16[8192]{0:T(1024)(128)(2,1)S(1)} %convert_element_type.25), channel_id=1, replica_groups=mesh['row'=4,'col'=64] {'col'}, use_global_device_ids=true, to_apply=%region_6.7 | all-reduce | flops 8192 | bytes 32768 | tf_op jit(solution)/shard_map/pmax | solution.py:42
  380.5 246.1 %psum.28 = f32[8192]{0:T(1024)S(1)} all-reduce(f32[8192]{0:T(1024)S(1)} %fusion.26), channel_id=1, replica_groups=mesh['row'=4,'col'=64] {'col'}, use_global_device_ids=true, to_apply=%region_7.8 | all-reduce | flops 8192 | bytes 65536 | tf_op jit(solution)/shard_map/psum | solution.py:43
  626.6 43.5 %while.39 = (s32[]{:T(128)}, f32[512]{0:T(512)S(1)}, f32[512]{0:T(512)S(1)}, f32[16,512]{1,0:T(8,128)S(1)}, bf16[16,512,128]{2,1,0:T(8,128)(2,1)}, /*index=5*/f3...) while((s32[]{:T(128)}, f32[512]{0:T(512)S(1)}, f32[512]{0:T(512)S(1)}, ...), condition=%wide.region_12.13_spmd.clone, body=%wide.region_8.12_spmd.clone.sunk | while | flops 69666816 | bytes 2529404 | solution.py:61
  627.7 1.4 fusion.55
  630.4 1.4 fusion.55
  633.2 1.4 fusion.55
  635.9 1.4 fusion.55
  638.6 1.4 fusion.55
  641.3 1.4 fusion.55
  644.0 1.4 fusion.55
  646.7 1.4 fusion.55
  649.5 1.4 fusion.55
  652.2 1.4 fusion.55
  654.9 1.4 fusion.55
  657.6 1.4 fusion.55
  660.3 1.4 fusion.55
  663.0 1.4 fusion.55
  665.7 1.4 fusion.55
  668.5 1.4 fusion.55
  670.1 8.3 pmax.15
  678.4 6.0 psum.29
  684.5 60.0 %while.38 = (s32[]{:T(128)}, f32[16,512,128]{2,1,0:T(8,128)}, f32[16,512]{1,0:T(8,128)S(1)}, f32[16,512]{1,0:T(8,128)S(1)}, f32[512]{0:T(512)S(1)}, /*index=5*/b...) while((s32[]{:T(128)}, f32[16,512,128]{2,1,0:T(8,128)}, ...), condition=%wide.region_18.19_spmd, body=%wide.region_15.18_spmd.sunk | while | flops 136772608 | bytes 2379933 | solution.py:80
  685.6 1.5 fusion.52
  689.3 1.5 fusion.52
  692.0 1.1 multiply_reduce_fusion.8
  693.1 1.5 fusion.52
  695.7 1.1 multiply_reduce_fusion.8
  696.8 1.5 fusion.52
  700.5 1.5 fusion.52
  703.2 1.1 multiply_reduce_fusion.8
  704.3 1.5 fusion.52
  708.1 1.5 fusion.52
  710.7 1.1 multiply_reduce_fusion.8
  711.8 1.5 fusion.52
  714.5 1.1 multiply_reduce_fusion.8
  715.6 1.5 fusion.52
  718.2 1.1 multiply_reduce_fusion.8
  719.3 1.5 fusion.52
  723.1 1.5 fusion.52
  726.8 1.5 fusion.52
  730.6 1.5 fusion.52
  734.3 1.5 fusion.52
  738.1 1.5 fusion.52
  741.8 1.5 fusion.52
  745.6 250.6 %psum.31 = f32[8192]{0:T(1024)S(1)} all-reduce(f32[8192]{0:T(1024)S(1)} %bitcast.84), channel_id=1, replica_groups=mesh['row'=4,'col'=64] {'col'}, use_global_device_ids=true, to_apply=%region_20.21 | all-reduce | flops 8192 | bytes 65536 | tf_op jit(solution)/shard_map/psum | solution.py:84
  996.3 1.5 divide_convert_fusion
  (275 shorter events, 74.6 us)
Async XLA Ops:
  7.2 85.2 %all-gather.2.cloned.1.call-start = ((), (), s32[]{:S(2)}) async-start(), calls=%async_computation | async-start | bytes 2129920 | tf_op jit(solution)/shard_map/all_gather | solution.py:26
  7.9 988.4 %all-reduce.2.cloned.1.call-start = ((), (), s32[]{:S(2)}) async-start(), calls=%async_computation.1 | async-start | bytes 8388608 | tf_op jit(solution)/shard_map/psum | solution.py:84
  684.5 2.7 copy-start
  688.2 2.7 copy-start
  691.9 2.7 copy-start
  695.7 2.7 copy-start
  699.4 2.7 copy-start
  703.2 2.7 copy-start
  707.0 2.7 copy-start
  710.7 2.7 copy-start
  714.4 2.7 copy-start
  718.2 2.7 copy-start
  722.0 2.7 copy-start
  725.7 2.7 copy-start
  729.5 2.7 copy-start
  733.2 2.7 copy-start
  737.0 2.7 copy-start
  740.7 2.7 copy-start
  744.5 0.6 copy-start.1
Sparse Core Ops, SparseCore 0:
  10.8 81.5 all-gather.1
  744.6 195.5 all-reduce.1
where the time goes:
time: 1010 us; the launch traced here: 1000 us
  blocking collectives  754 us (75%)
  matrix products  85.3 us (8%)
  waiting for transfers between devices  84 us (8%)
  other arithmetic  60.5 us (6%)
  between operations  14.1 us (1%)
    psum x1, blocking collectives, local(): full_num, full_den = lax.psum((numerator, denominator), 'col')  251 us
    psum x1, blocking collectives, local(): top_sum = lax.psum(row_sum * jnp.exp(row_peak - top_peak), 'col')  246 us
    pmax x1, blocking collectives, local(): lax.pmax(row_peak.astype(jnp.bfloat16), 'col').astype(row_peak.dtype)  243 us
    all_gather x1, waiting for transfers between devices, local(): gathered = lax.all_gather(source, 'col', axis=0, tiled=True)  83.3 us
    dot_general x48, matrix products, cost_tile(): lax.dot_general(block_rows, target, (((1,), (1,)), ((), ())), preferred_e...  68.4 us
    reduce_sum x48, other arithmetic, cost_tile(): row_sq = jnp.sum(jnp.square(block_rows.astype(jnp.float32)), axis=1)  51.2 us
  transfers between devices with their start and end apart: 2, of which 1 were waited for; matrix products, arithmetic and copies ran while one was open for 0% of the time, Pallas kernels for 0%

commit v1 on v0

v1 whole, which is shorter than its diff:
```python
import functools
import math

import jax
import jax.numpy as jnp
from jax import lax
from jax.experimental import pallas as pl
from jax.experimental.pallas import tpu as pltpu
from jax.sharding import PartitionSpec as P

MESH = pl.DeviceIdType.MESH
EPS = 0.02
LOG2E = 1.0 / math.log(2.0)
F32 = jnp.float32
BF16 = jnp.bfloat16

Y, Z, C = 4, 8, 2
LOW = -1e30
VMEM = 63495680
W, EXTRA = 128, 16


def split2(x):
    hi = x.astype(BF16)
    return hi, (x - hi.astype(F32)).astype(BF16)


def split3(x):
    hi = x.astype(BF16).astype(F32)
    mid = (x - hi).astype(BF16).astype(F32)
    return hi, mid, x - hi - mid


def squares(rows):
    both = jnp.concatenate(split2(jnp.square(rows.astype(F32))), axis=1)
    ones = jnp.ones((8, both.shape[1]), BF16)
    return lax.dot_general(ones, both, (((1,), (1,)), ((), ())), preferred_element_type=F32)[0:1, :]


def kernel(dims, src, tgt, pot, f_out, g_out, map_out, tbuf, abuf, sbuf, pbuf, lhs, rhs, ta, buf_a, buf_b, col_a, col_b, macc, sacc, lrow, lfin,
           mstage, sstage, mcol, lcol, xbuf, zsend, zbuf, wrep, e2, acc, nsend, nrecv, i_sem, a_send, a_recv, t_send, t_recv, s_send, s_recv,
           r_send, r_recv, x_send, x_recv, z_send, z_recv, n_send, n_recv):
    X, Y, Z, C, ns, nt, D, all_s, all_t = dims
    G = Y * C
    Q = nt // W
    CH = Z * W
    SCALE = LOG2E / (D * EPS)
    x = lax.axis_index("row")
    col = lax.axis_index("col")
    y = col // (Z * C)
    z = (col // C) % Z
    c = col % C

    def dev(xx, yy, zz, cc):
        return {"row": xx, "col": (yy * Z + zz) * C + cc}

    def remote(a, b, send, recv, to):
        cp = pltpu.make_async_remote_copy(
            src_ref=a, dst_ref=b, send_sem=send, recv_sem=recv, device_id=to, device_id_type=MESH)
        cp.start()
        return cp

    def lse(items):
        top = functools.reduce(jnp.maximum, items)
        total = functools.reduce(jnp.add, [jnp.exp2((i - top) * SCALE) for i in items])
        return top + jnp.log2(total) * (1.0 / SCALE)

    group = [(dy, dc) for dy in range(Y) for dc in range(C) if (dy, dc) != (0, 0)]

    def group_dev(dy, dc):
        return dev(x, (y + dy) % Y, z, (c + dc) % C)

    place = y * C + c

    barrier = pltpu.get_barrier_semaphore()
    peers = [group_dev(*g) for g in group]
    peers += [dev((x + d) % X, y, z, c) for d in range(1, X)]
    peers += [dev(x, y, (z + d) % Z, c) for d in range(1, Z)]
    for peer in peers:
        pl.semaphore_signal(barrier, inc=1, device_id=peer, device_id_type=MESH)
    fetch = [pltpu.make_async_copy(tgt.at[pl.ds(q * W, W), :], tbuf.at[0, q], i_sem.at[q]) for q in range(Q)]
    fetch.append(pltpu.make_async_copy(pot, pbuf, i_sem.at[Q]))
    fetch.append(pltpu.make_async_copy(src, sbuf.at[place], i_sem.at[Q + 1]))
    for cp in fetch:
        cp.start()
    pl.semaphore_wait(barrier, len(peers))

    s_copies = [remote(src, sbuf.at[place], s_send.at[i], s_recv.at[i], group_dev(*g)) for i, g in enumerate(group)]

    H = Z // 2
    t_copies = {}
    right = dev(x, y, (z + 1) % Z, c)
    left = dev(x, y, (z + Z - 1) % Z, c)

    def to_z(r, j):
        q = (x + j) % Q
        k = r * Q + j
        t_copies[r, j] = remote(
            tgt.at[pl.ds(pl.multiple_of(q * W, W), W), :], tbuf.at[r, q], t_send.at[k], t_recv.at[k],
            dev(x, y, (z + Z - r) % Z, c))

    for d in range(2, H):
        to_z(d, 0)
        to_z(Z - d, 0)
    for j in range(Q):
        to_z(1, j)
        to_z(Z - 1, j)

    def half_way():
        have = jnp.where(c == 0, H + 1, H - 1)
        to = jnp.where(c == 0, (z + 1) % Z, (z + Z - 1) % Z)
        k = H * Q
        t_copies[H, 0] = remote(tbuf.at[have, x], tbuf.at[H, x], t_send.at[k], t_recv.at[k], dev(x, y, to, c))

    def spread(r):
        t_copies[r, 0].wait_recv()
        for d in range(1, X):
            k = r * Q + d
            t_copies[r, d] = remote(tbuf.at[r, x], tbuf.at[r, x], t_send.at[k], t_recv.at[k], dev((x + d) % X, y, z, c))

    for cp in fetch:
        cp.wait()
    own_sq = [squares(tbuf[0, q]) for q in range(Q)]
    offset = jnp.concatenate([pbuf[0:1, q * W:(q + 1) * W] * float(D) - 0.5 * own_sq[q] for q in range(Q)], axis=0)
    abuf[0] = jnp.concatenate(list(split3(offset)) + [jnp.zeros((EXTRA - 3 * Q, W), F32)], axis=0).astype(BF16)
    a_copies = [
        remote(abuf.at[0], abuf.at[r], a_send.at[r - 1], a_recv.at[r - 1], dev(x, y, (z + Z - r) % Z, c)) for r in range(1, Z)]

    rhs[D + EXTRA:2 * D, :] = jnp.zeros((D - EXTRA, Z * nt), BF16)
    macc[...] = jnp.full(macc.shape, LOW, F32)
    sacc[...] = jnp.zeros(sacc.shape, F32)
    lanes = lax.broadcasted_iota(jnp.int32, (ns, D), 1)
    for cp in s_copies:
        cp.wait_recv()
    for p in range(G):
        lhs[p * ns:(p + 1) * ns, 0:D] = sbuf[p]
        lhs[p * ns:(p + 1) * ns, D:2 * D] = jnp.where(lanes < 3, 1.0, 0.0).astype(BF16)

    def take(slot):
        offsets = abuf[slot].astype(F32)
        for q in range(Q):
            at = q * CH + slot * W
            piece = tbuf[slot, q]
            rhs[0:D, at:at + W] = piece.T
            rhs[D:D + EXTRA, at:at + W] = jnp.concatenate(
                [offsets[q + i * Q:q + i * Q + 1, :] for i in range(3)]
                + [jnp.ones((3, W), F32), jnp.zeros((EXTRA - 6, W), F32)], axis=0).astype(BF16)
            ta[at:at + W, 0:D] = piece
            ta[at:at + W, D:2 * D] = jnp.ones((W, D), BF16)

    step = 2 * ns

    def fold(buf, start):
        for i in range(step // 64):
            rows = pl.ds(start + i * 64, 64)
            pieces = [buf[i * 64:(i + 1) * 64, q * W:(q + 1) * W] for q in range(Q)]
            old = macc[rows, :]
            top = functools.reduce(jnp.maximum, pieces, old)
            total = sacc[rows, :] * jnp.exp2((old - top) * SCALE)
            for piece in pieces:
                total = total + jnp.exp2((piece - top) * SCALE)
            macc[rows, :] = top
            sacc[rows, :] = total

    def row_pass(slot):
        @pl.loop(0, G // 4)
        def _(p):
            right_side = jnp.concatenate([rhs[:, q * CH + slot * W:q * CH + (slot + 1) * W] for q in range(Q)], axis=1)
            first = pl.multiple_of(p * 2 * step, 2 * step)
            second = pl.multiple_of(p * 2 * step + step, step)
            buf_a[...] = jnp.dot(lhs[pl.ds(first, step), :], right_side, preferred_element_type=F32)
            buf_b[...] = jnp.dot(lhs[pl.ds(second, step), :], right_side, preferred_element_type=F32)
            fold(buf_a, first)
            fold(buf_b, second)

    def arrive(slot):
        a_copies[slot - 1].wait_recv()
        for j in range(Q):
            if j > 0 or slot in (1, Z - 1):
                t_copies[slot, j].wait_recv()
        take(slot)
        row_pass(slot)

    take(0)
    row_pass(0)
    for d in range(2, H):
        spread(d)
        spread(Z - d)
    half_way()
    arrive(1)
    spread(H)
    arrive(Z - 1)
    for d in range(2, H):
        arrive(d)
        arrive(Z - d)
    arrive(H)

    for p in range(G):
        m = macc[p * ns:(p + 1) * ns, :].T
        s = sacc[p * ns:(p + 1) * ns, :].T
        top = jnp.max(m, axis=0, keepdims=True)
        total = jnp.sum(s * jnp.exp2((m - top) * SCALE), axis=0, keepdims=True)
        lrow[0, p:p + 1, :] = top + jnp.log2(total) * (1.0 / SCALE)
    r_copies = [
        remote(lrow.at[0], lrow.at[i + 1], r_send.at[i], r_recv.at[i], group_dev(*g)) for i, g in enumerate(group)]
    src_sq = squares(sbuf[place])
    for cp in r_copies:
        cp.wait_recv()
    l1 = lse([lrow[i] for i in range(G)])
    lfin[0:G, :] = l1
    for p in range(G):
        parts = [jnp.zeros((3, ns), F32)] + list(split3(-l1[p:p + 1, :])) + [jnp.zeros((D - 6, ns), F32)]
        lhs[p * ns:(p + 1) * ns, D:2 * D] = jnp.concatenate(parts, axis=0).T.astype(BF16)
    f_out[...] = (0.5 * src_sq - lfin[pl.ds(place, 1), :]) * (1.0 / D) - EPS * math.log(all_s)

    def scores(buf, at):
        buf[...] = jnp.dot(lhs[...], rhs[:, pl.ds(pl.multiple_of(at, 2 * W), 2 * W)], preferred_element_type=F32)

    def column(buf, slot, at):
        for i in range(2):
            wide = slice(i * W, (i + 1) * W)
            top = buf[0:64, wide]
            for j in range(1, G * ns // 64):
                top = jnp.maximum(top, buf[j * 64:(j + 1) * 64, wide])
            top = jnp.max(top, axis=0, keepdims=True)
            total = jnp.zeros((64, W), F32)
            for j in range(G * ns // 64):
                e = jnp.exp2((buf[j * 64:(j + 1) * 64, wide] - top) * SCALE)
                total = total + e
                e2[j * 64:(j + 1) * 64, pl.ds(pl.multiple_of(at + i * W, W), W)] = e.astype(BF16)
            total = jnp.sum(total, axis=0, keepdims=True)
            mstage[slot + i] = jnp.broadcast_to(top, (8, W))
            sstage[slot + i] = jnp.broadcast_to(total, (8, W))

    x_copies, z_copies = {}, {}

    def column_chunk(q):
        scores(col_a, q * CH)

        @pl.loop(0, Z // 4)
        def _(t):
            slot = t * 4
            at = q * CH + slot * W
            scores(col_b, at + 2 * W)
            column(col_a, slot, at)
            scores(col_a, jnp.minimum(at + 4 * W, (q + 1) * CH - 2 * W))
            column(col_b, slot + 2, at + 2 * W)

        mcol[q] = jnp.concatenate([mstage[r, 0:1, :] for r in range(Z)], axis=0)
        total = jnp.concatenate([sstage[r, 0:1, :] for r in range(Z)], axis=0)
        lcol[q] = mcol[q] + jnp.log2(total) * (1.0 / SCALE)
        for d in range(1, X):
            k = q * (X - 1) + d - 1
            x_copies[q, d] = remote(lcol.at[q], xbuf.at[k], x_send.at[k], x_recv.at[k], dev((x + d) % X, y, z, c))

    def across_z(q):
        for d in range(1, X):
            x_copies[q, d].wait_recv()
        zsend[q] = lse([lcol[q]] + [xbuf[q * (X - 1) + d - 1] for d in range(1, X)])
        for d in range(1, Z):
            k = q * (Z - 1) + d - 1
            z_copies[q, d] = remote(zsend.at[q], zbuf.at[k], z_send.at[k], z_recv.at[k], dev(x, y, (z + d) % Z, c))

    def weights(q):
        terms = [zsend[q]]
        for d in range(1, Z):
            z_copies[q, d].wait_recv()
            got = zbuf[q * (Z - 1) + d - 1]
            terms.append(jnp.concatenate([got[d:Z, :], got[0:d, :]], axis=0))
        l2 = lse(terms)
        g_out[0:1, q * W:(q + 1) * W] = (0.5 * own_sq[q] - l2[0:1, :]) * (1.0 / D) + EPS * (math.log(all_s) - math.log(all_t))
        w = jnp.exp2((mcol[q] - l2) * SCALE)
        for r in range(Z):
            wrep[q, :, r * W:(r + 1) * W] = jnp.broadcast_to(w[r:r + 1, :], (16, W)).astype(BF16)

    pair = C * ns

    def weighted(q, start):
        plan = e2[pl.ds(start, pair), q * CH:(q + 1) * CH]
        plan = (plan.reshape(pair // 16, 16, CH) * wrep[q][None]).reshape(pair, CH)
        return jnp.dot(plan, ta[q * CH:(q + 1) * CH, :], preferred_element_type=F32)

    def add_chunk(q):
        weights(q)

        @pl.loop(0, Y)
        def _(t):
            start = pl.multiple_of(t * pair, pair)
            got = weighted(q, start)
            acc[pl.ds(start, pair), :] = got if q == 0 else acc[pl.ds(start, pair), :] + got

    for q in range(Q):
        column_chunk(q)
        if q > 0:
            across_z(q - 1)
    add_chunk(0)
    across_z(Q - 1)
    for q in range(1, Q - 1):
        add_chunk(q)
    weights(Q - 1)

    eye = lax.broadcasted_iota(jnp.int32, (ns, W), 0) == lax.broadcasted_iota(jnp.int32, (ns, W), 1)
    n_copies = {}
    own = None
    for dy in sorted(range(1, Y), key=lambda d: -min(d, Y - d)) + [0]:
        start = pl.multiple_of(((y + dy) % Y) * pair, pair)
        acc[pl.ds(start, pair), :] = acc[pl.ds(start, pair), :] + weighted(Q - 1, start)
        for dc in reversed(range(C)):
            rows = pl.ds(pl.multiple_of(start + ((c + dc) % C) * ns, ns), ns)
            num, den = acc[rows, 0:D], acc[rows, D:2 * D]
            den = jnp.sum(jnp.where(eye, den, 0.0), axis=0, keepdims=True)
            if (dy, dc) == (0, 0):
                own = (num, den)
                continue
            i = group.index((dy, dc))
            hi, lo = split2(den)
            nsend[i, 0:ns, :] = num.astype(BF16)
            nsend[i, ns:ns + 16, :] = jnp.concatenate(
                [hi.astype(F32), lo.astype(F32), jnp.zeros((14, W), F32)], axis=0).astype(BF16)
            n_copies[i] = remote(nsend.at[i], nrecv.at[i], n_send.at[i], n_recv.at[i], group_dev(dy, dc))
    for cps in (s_copies, a_copies, t_copies.values(), r_copies, x_copies.values(), z_copies.values()):
        for cp in cps:
            cp.wait_send()
    num, den = own
    for i in n_copies:
        n_copies[i].wait_recv()
        got = nrecv[i].astype(F32)
        num = num + got[0:ns, :]
        den = den + got[ns:ns + 1, :] + got[ns + 1:ns + 2, :]
    den = jnp.broadcast_to(den, (ns, W)).T
    map_out[...] = (num / den).astype(BF16)
    for cp in n_copies.values():
        cp.wait_send()


def local(dims, source, target, potential):
    X, Y, Z, C, ns, nt, D, all_s, all_t = dims
    G = Y * C
    Q = nt // W
    vm = pltpu.VMEM
    dma = pltpu.SemaphoreType.DMA
    f, g, mapped = pl.pallas_call(
        functools.partial(kernel, dims),
        out_shape=(
            jax.ShapeDtypeStruct((1, ns), F32),
            jax.ShapeDtypeStruct((1, nt), F32),
            jax.ShapeDtypeStruct((ns, D), BF16),
        ),
        in_specs=[pl.BlockSpec(memory_space=pl.ANY)] * 3,
        out_specs=(pl.BlockSpec(memory_space=pltpu.VMEM),) * 3,
        scratch_shapes=[
            vm((Z, Q, W, D), BF16),
            vm((Z, EXTRA, W), BF16),
            vm((G, ns, D), BF16),
            vm((1, nt), F32),
            vm((G * ns, 2 * D), BF16),
            vm((2 * D, Z * nt), BF16),
            vm((Z * nt, 2 * D), BF16),
            vm((2 * ns, nt), F32),
            vm((2 * ns, nt), F32),
            vm((G * ns, 2 * W), F32),
            vm((G * ns, 2 * W), F32),
            vm((G * ns, 128), F32),
            vm((G * ns, 128), F32),
            vm((G, G, ns), F32),
            vm((8, ns), F32),
            vm((Z, 8, W), F32),
            vm((Z, 8, W), F32),
            vm((Q, Z, W), F32),
            vm((Q, Z, W), F32),
            vm((Q * (X - 1), Z, W), F32),
            vm((Q, Z, W), F32),
            vm((Q * (Z - 1), Z, W), F32),
            vm((Q, 16, Z * W), BF16),
            vm((G * ns, Z * nt), BF16),
            vm((G * ns, 2 * D), F32),
            vm((G - 1, ns + 16, D), BF16),
            vm((G - 1, ns + 16, D), BF16),
            dma((Q + 2,)),
            dma((Z - 1,)), dma((Z - 1,)),
            dma((Z * Q,)), dma((Z * Q,)),
            dma((G - 1,)), dma((G - 1,)),
            dma((G - 1,)), dma((G - 1,)),
            dma((Q * (X - 1),)), dma((Q * (X - 1),)),
            dma((Q * (Z - 1),)), dma((Q * (Z - 1),)),
            dma((G - 1,)), dma((G - 1,)),
        ],
        compiler_params=pltpu.CompilerParams(
            collective_id=0, has_side_effects=True, vmem_limit_bytes=VMEM),
        cost_estimate=pl.CostEstimate(flops=6 * 10**9, bytes_accessed=10**6, transcendentals=10**7),
    )(source, target, potential.reshape(1, nt))
    return f.reshape(ns), g.reshape(nt), mapped


def solution(mesh, shape=(Y, Z, C)):
    placed = (P(("row", "col"), None), P("col", None), P("col"))

    def whole(source, target, potential):
        rows, cols = mesh.shape["row"], mesh.shape["col"]
        dims = (rows, *shape, source.shape[0] // (rows * cols), target.shape[0] // cols, source.shape[1],
                source.shape[0], target.shape[0])
        return jax.shard_map(
            functools.partial(local, dims),
            mesh=mesh,
            in_specs=placed,
            out_specs=(P(("row", "col")), P("col"), P(("row", "col"), None)),
            check_vma=False,
        )(source, target, potential)

    return whole
```

time: 1010 us -> 59.8 us (0.06)
  blocking collectives: 754 us -> 0 us
  matrix products: 85.3 us -> 0 us
  waiting for transfers between devices: 84 us -> 0 us
  other arithmetic: 60.5 us -> 0 us
  Pallas kernels: 0 us -> 55.9 us
  between operations: 14.1 us -> 0.66 us
    psum x3 -> x0, blocking collectives: 503 us -> none  [the longest x1 251 us: local(): full_num, full_den = lax.psum((numerator, denominator), 'col')]
    pmax x2 -> x0, blocking collectives: 252 us -> none  [the longest x1 243 us: local(): lax.pmax(row_peak.astype(jnp.bfloat16), 'col').astype(row_peak.dtype)]
    dot_general x64 -> x0, matrix products: 85.3 us -> none  [the longest x48 68.4 us: cost_tile(): lax.dot_general(block_rows, target, (((1,), (1,)), ((), ())), preferred_e...]
    all_gather x1 -> x0, waiting for transfers between devices: 83.3 us -> none  [local(): gathered = lax.all_gather(source, 'col', axis=0, tiled=True)]
    reduce_sum x81 -> x0, other arithmetic: 58.5 us -> none  [the longest x48 51.2 us: cost_tile(): row_sq = jnp.sum(jnp.square(block_rows.astype(jnp.float32)), axis=1)]
    pallas_call x0 -> x1, Pallas kernels: none -> 55.9 us  [local(): pl.pallas_call(functools.partial(kernel, dims), out_shape=(jax.ShapeDtype...]
  transfers between devices with their start and end apart: 2 -> 0, of which waited for: 1 -> 0; matrix products, arithmetic and copies ran while one was open for 0% -> 0% of each run, Pallas kernels for 0% -> 0%
where the time goes in v1:
time: 59.8 us; the launch traced here: 59.6 us
  Pallas kernels  55.9 us (93%)
  local copies, waits for them, and re-layouts  3.05 us (5%)
  between operations  0.66 us (1%)
    pallas_call x1, Pallas kernels, local(): pl.pallas_call(functools.partial(kernel, dims), out_shape=(jax.ShapeDtype...  55.9 us
    unnamed x7, local copies, waits for them, and re-layouts  3.05 us

profile of v1, /device:TPU:1, one launch (start us, length us, event | category | flops | bytes accessed | tf_op | source)
XLA Modules:
  0.0 59.6 jit_solution(14401013627042226446)
XLA Ops:
  0.6 55.9 %shard_map.58 = (f32[1,128]{1,0:T(1,128)}, f32[1,512]{1,0:T(1,128)}, bf16[128,128]{1,0:T(8,128)(2,1)}) custom-call(bf16[128,128]{1,0:T(8,128)(2,1)} %src.1, bf16[512,128]{1,0:T(8,128)(2,1)} %tgt.1, f32[1,512]{1,0:T(1,128)} %bitcast.4), custom_call_target="tpu_custom_call" | custom-call | flops 6000000000 | bytes 1000000 | tf_op jit(solution)/shard_map/pallas_call | solution.py:342
  56.5 0.0 copy-start.1
  56.5 0.0 copy-start
  56.5 0.6 copy-done.1
  57.1 0.5 copy.9
  57.6 0.0 copy-done
  57.6 0.6 copy.10
  58.2 1.4 %copy.11 = bf16[128,128]{1,0:T(8,128)(2,1)} copy(bf16[128,128]{1,0:T(8,128)(2,1)} %get-tuple-element.14) | data formatting | bytes 65536
Async XLA Ops:
  56.5 0.6 %copy-start.1 = (f32[1,128]{1,0:T(1,128)S(1)}, f32[1,128]{1,0:T(1,128)}, u32[]{:S(2)}) copy-start(f32[1,128]{1,0:T(1,128)} %get-tuple-element.6) | copy-start | bytes 1540
  56.5 1.1 %copy-start = (f32[1,512]{1,0:T(1,128)S(1)}, f32[1,512]{1,0:T(1,128)}, u32[]{:S(2)}) copy-start(f32[1,512]{1,0:T(1,128)} %get-tuple-element.7) | copy-start | bytes 6148

commit v2 on v1

--- a/solution.py
+++ b/solution.py
@@ -16,7 +16,7 @@
 
 Y, Z, C = 4, 8, 2
 LOW = -1e30
-VMEM = 63495680
+VMEM = 63532032
 W, EXTRA = 128, 16
 
 
@@ -37,7 +37,7 @@
     return lax.dot_general(ones, both, (((1,), (1,)), ((), ())), preferred_element_type=F32)[0:1, :]
 
 
-def kernel(dims, src, tgt, pot, f_out, g_out, map_out, tbuf, abuf, sbuf, pbuf, lhs, rhs, ta, buf_a, buf_b, col_a, col_b, macc, sacc, lrow, lfin,
+def kernel(dims, src, tgt, pot, f_out, g_out, map_out, tbuf, abuf, sbuf, pbuf, lhs, rhs, ta, buf_a, buf_b, col_a, col_b, top_a, top_b, macc, sacc, lrow, lfin,
            mstage, sstage, mcol, lcol, xbuf, zsend, zbuf, wrep, e2, acc, nsend, nrecv, i_sem, a_send, a_recv, t_send, t_recv, s_send, s_recv,
            r_send, r_recv, x_send, x_recv, z_send, z_recv, n_send, n_recv):
     X, Y, Z, C, ns, nt, D, all_s, all_t = dims
@@ -78,122 +78,135 @@
     peers += [dev(x, y, (z + d) % Z, c) for d in range(1, Z)]
     for peer in peers:
         pl.semaphore_signal(barrier, inc=1, device_id=peer, device_id_type=MESH)
-    fetch = [pltpu.make_async_copy(tgt.at[pl.ds(q * W, W), :], tbuf.at[0, q], i_sem.at[q]) for q in range(Q)]
+    fetch = [pltpu.make_async_copy(tgt.at[pl.ds(q * W, W), :], tbuf.at[0, pl.ds(q * W, W), :], i_sem.at[q]) for q in range(Q)]
     fetch.append(pltpu.make_async_copy(pot, pbuf, i_sem.at[Q]))
     fetch.append(pltpu.make_async_copy(src, sbuf.at[place], i_sem.at[Q + 1]))
     for cp in fetch:
         cp.start()
+    rhs[D + EXTRA:2 * D, :] = jnp.zeros((D - EXTRA, Z * nt), BF16)
+    macc[...] = jnp.full(macc.shape, LOW, F32)
+    sacc[...] = jnp.zeros(sacc.shape, F32)
+    ta[:, D:2 * D] = jnp.ones((Z * nt, D), BF16)
+    lanes = lax.broadcasted_iota(jnp.int32, (ns, D), 1)
+    for p in range(G):
+        lhs[p * ns:(p + 1) * ns, D:2 * D] = jnp.where(lanes < 3, 1.0, 0.0).astype(BF16)
     pl.semaphore_wait(barrier, len(peers))
 
-    s_copies = [remote(src, sbuf.at[place], s_send.at[i], s_recv.at[i], group_dev(*g)) for i, g in enumerate(group)]
-
     H = Z // 2
+    half = nt // 2
     t_copies = {}
-    right = dev(x, y, (z + 1) % Z, c)
-    left = dev(x, y, (z + Z - 1) % Z, c)
-
-    def to_z(r, j):
-        q = (x + j) % Q
-        k = r * Q + j
-        t_copies[r, j] = remote(
-            tgt.at[pl.ds(pl.multiple_of(q * W, W), W), :], tbuf.at[r, q], t_send.at[k], t_recv.at[k],
-            dev(x, y, (z + Z - r) % Z, c))
-
-    for d in range(2, H):
-        to_z(d, 0)
-        to_z(Z - d, 0)
-    for j in range(Q):
-        to_z(1, j)
-        to_z(Z - 1, j)
+
+    def side(d):
+        return dev(x, y, (z + d) % Z, c)
+
+    own_piece = pl.ds(pl.multiple_of(x * W, W), W)
+
+    def to_z(r, k, a, b):
+        t_copies[r, k] = remote(a, b, t_send.at[r * Q + k], t_recv.at[r * Q + k], side(Z - r))
+
+    for r in (3, Z - 3):
+        to_z(r, 0, tgt.at[own_piece, :], tbuf.at[r, own_piece, :])
+    for h in range(2):
+        rows = pl.ds(h * half, half)
+        for r in (1, Z - 1):
+            to_z(r, h, tgt.at[rows, :], tbuf.at[r, rows, :])
+
+    def pass_on(r, h):
+        t_copies[r, h].wait_recv()
+        rows = pl.ds(h * half, half)
+        there = 2 if r == 1 else Z - 2
+        t_copies[there, h] = remote(
+            tbuf.at[r, rows, :], tbuf.at[there, rows, :], t_send.at[there * Q + h], t_recv.at[there * Q + h],
+            side(Z - 1 if r == 1 else 1))
 
     def half_way():
-        have = jnp.where(c == 0, H + 1, H - 1)
+        have = jnp.where(c == 0, Z - 3, 3)
         to = jnp.where(c == 0, (z + 1) % Z, (z + Z - 1) % Z)
-        k = H * Q
-        t_copies[H, 0] = remote(tbuf.at[have, x], tbuf.at[H, x], t_send.at[k], t_recv.at[k], dev(x, y, to, c))
+        t_copies[H, 0] = remote(
+            tbuf.at[have, own_piece, :], tbuf.at[H, own_piece, :], t_send.at[H * Q], t_recv.at[H * Q], dev(x, y, to, c))
 
     def spread(r):
         t_copies[r, 0].wait_recv()
         for d in range(1, X):
             k = r * Q + d
-            t_copies[r, d] = remote(tbuf.at[r, x], tbuf.at[r, x], t_send.at[k], t_recv.at[k], dev((x + d) % X, y, z, c))
+            t_copies[r, d] = remote(
+                tbuf.at[r, own_piece, :], tbuf.at[r, own_piece, :], t_send.at[k], t_recv.at[k], dev((x + d) % X, y, z, c))
+
+    s_copies = [remote(src, sbuf.at[place], s_send.at[i], s_recv.at[i], group_dev(*g)) for i, g in enumerate(group)]
 
     for cp in fetch:
         cp.wait()
-    own_sq = [squares(tbuf[0, q]) for q in range(Q)]
+    own_sq = [squares(tbuf[0, q * W:(q + 1) * W, :]) for q in range(Q)]
     offset = jnp.concatenate([pbuf[0:1, q * W:(q + 1) * W] * float(D) - 0.5 * own_sq[q] for q in range(Q)], axis=0)
     abuf[0] = jnp.concatenate(list(split3(offset)) + [jnp.zeros((EXTRA - 3 * Q, W), F32)], axis=0).astype(BF16)
     a_copies = [
         remote(abuf.at[0], abuf.at[r], a_send.at[r - 1], a_recv.at[r - 1], dev(x, y, (z + Z - r) % Z, c)) for r in range(1, Z)]
 
-    rhs[D + EXTRA:2 * D, :] = jnp.zeros((D - EXTRA, Z * nt), BF16)
-    macc[...] = jnp.full(macc.shape, LOW, F32)
-    sacc[...] = jnp.zeros(sacc.shape, F32)
-    lanes = lax.broadcasted_iota(jnp.int32, (ns, D), 1)
+    spread(3)
+    spread(Z - 3)
+    half_way()
+
     for cp in s_copies:
         cp.wait_recv()
     for p in range(G):
         lhs[p * ns:(p + 1) * ns, 0:D] = sbuf[p]
-        lhs[p * ns:(p + 1) * ns, D:2 * D] = jnp.where(lanes < 3, 1.0, 0.0).astype(BF16)
 
     def take(slot):
         offsets = abuf[slot].astype(F32)
         for q in range(Q):
             at = q * CH + slot * W
-            piece = tbuf[slot, q]
+            piece = tbuf[slot, q * W:(q + 1) * W, :]
             rhs[0:D, at:at + W] = piece.T
             rhs[D:D + EXTRA, at:at + W] = jnp.concatenate(
                 [offsets[q + i * Q:q + i * Q + 1, :] for i in range(3)]
                 + [jnp.ones((3, W), F32), jnp.zeros((EXTRA - 6, W), F32)], axis=0).astype(BF16)
             ta[at:at + W, 0:D] = piece
-            ta[at:at + W, D:2 * D] = jnp.ones((W, D), BF16)
-
-    step = 2 * ns
+
+    RC = 64
+    per = G * ns // 2 // RC
 
     def fold(buf, start):
-        for i in range(step // 64):
-            rows = pl.ds(start + i * 64, 64)
-            pieces = [buf[i * 64:(i + 1) * 64, q * W:(q + 1) * W] for q in range(Q)]
-            old = macc[rows, :]
-            top = functools.reduce(jnp.maximum, pieces, old)
-            total = sacc[rows, :] * jnp.exp2((old - top) * SCALE)
-            for piece in pieces:
-                total = total + jnp.exp2((piece - top) * SCALE)
-            macc[rows, :] = top
-            sacc[rows, :] = total
+        rows = pl.ds(start, RC)
+        pieces = [buf[:, q * W:(q + 1) * W] for q in range(Q)]
+        old = macc[rows, :]
+        top = functools.reduce(jnp.maximum, pieces, old)
+        total = sacc[rows, :] * jnp.exp2((old - top) * SCALE)
+        for piece in pieces:
+            total = total + jnp.exp2((piece - top) * SCALE)
+        macc[rows, :] = top
+        sacc[rows, :] = total
 
     def row_pass(slot):
-        @pl.loop(0, G // 4)
+        @pl.loop(0, 2)
         def _(p):
             right_side = jnp.concatenate([rhs[:, q * CH + slot * W:q * CH + (slot + 1) * W] for q in range(Q)], axis=1)
-            first = pl.multiple_of(p * 2 * step, 2 * step)
-            second = pl.multiple_of(p * 2 * step + step, step)
-            buf_a[...] = jnp.dot(lhs[pl.ds(first, step), :], right_side, preferred_element_type=F32)
-            buf_b[...] = jnp.dot(lhs[pl.ds(second, step), :], right_side, preferred_element_type=F32)
-            fold(buf_a, first)
-            fold(buf_b, second)
+            start = pl.multiple_of(p * per * RC, per * RC)
+            bufs = (buf_a, buf_b)
+            for i in range(per + 1):
+                if i < per:
+                    bufs[i % 2][...] = jnp.dot(lhs[pl.ds(start + i * RC, RC), :], right_side, preferred_element_type=F32)
+                if i > 0:
+                    fold(bufs[(i - 1) % 2], start + (i - 1) * RC)
+
+    waited = {(1, 0), (1, 1), (Z - 1, 0), (Z - 1, 1), (3, 0), (Z - 3, 0), (H, 0)}
 
     def arrive(slot):
         a_copies[slot - 1].wait_recv()
-        for j in range(Q):
-            if j > 0 or slot in (1, Z - 1):
-                t_copies[slot, j].wait_recv()
+        for (r, k), cp in t_copies.items():
+            if r == slot and (r, k) not in waited:
+                cp.wait_recv()
         take(slot)
         row_pass(slot)
 
     take(0)
+    pass_on(1, 0)
+    pass_on(Z - 1, 0)
     row_pass(0)
-    for d in range(2, H):
-        spread(d)
-        spread(Z - d)
-    half_way()
-    arrive(1)
     spread(H)
-    arrive(Z - 1)
-    for d in range(2, H):
-        arrive(d)
-        arrive(Z - d)
-    arrive(H)
+    pass_on(1, 1)
+    pass_on(Z - 1, 1)
+    for slot in (1, Z - 1, 3, Z - 3, 2, Z - 2, H):
+        arrive(slot)
 
     for p in range(G):
         m = macc[p * ns:(p + 1) * ns, :].T
@@ -213,38 +226,51 @@
         lhs[p * ns:(p + 1) * ns, D:2 * D] = jnp.concatenate(parts, axis=0).T.astype(BF16)
     f_out[...] = (0.5 * src_sq - lfin[pl.ds(place, 1), :]) * (1.0 / D) - EPS * math.log(all_s)
 
-    def scores(buf, at):
-        buf[...] = jnp.dot(lhs[...], rhs[:, pl.ds(pl.multiple_of(at, 2 * W), 2 * W)], preferred_element_type=F32)
-
-    def column(buf, slot, at):
+    MC = 128
+    chunks = G * ns // MC
+
+    def scores(buf, tops, at):
+        right_side = rhs[:, pl.ds(pl.multiple_of(at, 2 * W), 2 * W)]
+        top = None
+        for i in range(chunks):
+            u = jnp.dot(lhs[i * MC:(i + 1) * MC, :], right_side, preferred_element_type=F32)
+            buf[i * MC:(i + 1) * MC, :] = u
+            part = jnp.max(u.reshape(MC // 8, 8, 2 * W), axis=0)
+            top = part if top is None else jnp.maximum(top, part)
+            yield
+        tops[...] = jnp.broadcast_to(jnp.max(top, axis=0, keepdims=True), (8, 2 * W))
+        yield
+
+    def column(buf, tops, slot, at):
+        top = tops[...]
+        total = jnp.zeros((8, 2 * W), F32)
+        for i in range(chunks):
+            for j in range(0, MC, 32):
+                rows = slice(i * MC + j, i * MC + j + 32)
+                e = jnp.exp2((buf[rows, :].reshape(4, 8, 2 * W) - top[None]) * SCALE)
+                total = total + jnp.sum(e, axis=0)
+                e2[rows, pl.ds(pl.multiple_of(at, 2 * W), 2 * W)] = e.reshape(32, 2 * W).astype(BF16)
+            yield
+        total = jnp.broadcast_to(jnp.sum(total, axis=0, keepdims=True), (8, 2 * W))
         for i in range(2):
-            wide = slice(i * W, (i + 1) * W)
-            top = buf[0:64, wide]
-            for j in range(1, G * ns // 64):
-                top = jnp.maximum(top, buf[j * 64:(j + 1) * 64, wide])
-            top = jnp.max(top, axis=0, keepdims=True)
-            total = jnp.zeros((64, W), F32)
-            for j in range(G * ns // 64):
-                e = jnp.exp2((buf[j * 64:(j + 1) * 64, wide] - top) * SCALE)
-                total = total + e
-                e2[j * 64:(j + 1) * 64, pl.ds(pl.multiple_of(at + i * W, W), W)] = e.astype(BF16)
-            total = jnp.sum(total, axis=0, keepdims=True)
-            mstage[slot + i] = jnp.broadcast_to(top, (8, W))
-            sstage[slot + i] = jnp.broadcast_to(total, (8, W))
+            mstage[slot + i] = top[:, i * W:(i + 1) * W]
+            sstage[slot + i] = total[:, i * W:(i + 1) * W]
+        yield
+
+    def together(*steps):
+        for _ in zip(*steps):
+            pass
 
     x_copies, z_copies = {}, {}
 
     def column_chunk(q):
-        scores(col_a, q * CH)
-
         @pl.loop(0, Z // 4)
         def _(t):
             slot = t * 4
             at = q * CH + slot * W
-            scores(col_b, at + 2 * W)
-            column(col_a, slot, at)
-            scores(col_a, jnp.minimum(at + 4 * W, (q + 1) * CH - 2 * W))
-            column(col_b, slot + 2, at + 2 * W)
+            together(scores(col_b, top_b, at + 2 * W), column(col_a, top_a, slot, at))
+            after = at + 4 * W if q < Q - 1 else jnp.minimum(at + 4 * W, Z * nt - 2 * W)
+            together(scores(col_a, top_a, after), column(col_b, top_b, slot + 2, at + 2 * W))
 
         mcol[q] = jnp.concatenate([mstage[r, 0:1, :] for r in range(Z)], axis=0)
         total = jnp.concatenate([sstage[r, 0:1, :] for r in range(Z)], axis=0)
@@ -275,20 +301,26 @@
 
     pair = C * ns
 
-    def weighted(q, start):
-        plan = e2[pl.ds(start, pair), q * CH:(q + 1) * CH]
-        plan = (plan.reshape(pair // 16, 16, CH) * wrep[q][None]).reshape(pair, CH)
-        return jnp.dot(plan, ta[q * CH:(q + 1) * CH, :], preferred_element_type=F32)
+    KC = CH // 2
+
+    def weighted(q, start, first):
+        for i in range(0, pair, MC):
+            rows = pl.ds(start + i, MC)
+            total = None if first else acc[rows, :]
+            for k in range(0, CH, KC):
+                plan = e2[rows, q * CH + k:q * CH + k + KC].reshape(MC // 16, 16, KC) * wrep[q, :, k:k + KC][None]
+                got = jnp.dot(plan.reshape(MC, KC), ta[q * CH + k:q * CH + k + KC, :], preferred_element_type=F32)
+                total = got if total is None else total + got
+            acc[rows, :] = total
 
     def add_chunk(q):
         weights(q)
 
         @pl.loop(0, Y)
         def _(t):
-            start = pl.multiple_of(t * pair, pair)
-            got = weighted(q, start)
-            acc[pl.ds(start, pair), :] = got if q == 0 else acc[pl.ds(start, pair), :] + got
-
+            weighted(q, pl.multiple_of(t * pair, pair), q == 0)
+
+    together(scores(col_a, top_a, 0))
     for q in range(Q):
         column_chunk(q)
         if q > 0:
@@ -304,7 +336,7 @@
     own = None
     for dy in sorted(range(1, Y), key=lambda d: -min(d, Y - d)) + [0]:
         start = pl.multiple_of(((y + dy) % Y) * pair, pair)
-        acc[pl.ds(start, pair), :] = acc[pl.ds(start, pair), :] + weighted(Q - 1, start)
+        weighted(Q - 1, start, False)
         for dc in reversed(range(C)):
             rows = pl.ds(pl.multiple_of(start + ((c + dc) % C) * ns, ns), ns)
             num, den = acc[rows, 0:D], acc[rows, D:2 * D]
@@ -333,6 +365,15 @@
         cp.wait_send()
 
 
+def write_out(f, g, mapped, f_out, g_out, map_out, sem):
+    copies = [
+        pltpu.make_async_copy(a, b, sem.at[i]) for i, (a, b) in enumerate(((f, f_out), (g, g_out), (mapped, map_out)))]
+    for cp in copies:
+        cp.start()
+    for cp in copies:
+        cp.wait()
+
+
 def local(dims, source, target, potential):
     X, Y, Z, C, ns, nt, D, all_s, all_t = dims
     G = Y * C
@@ -349,17 +390,19 @@
         in_specs=[pl.BlockSpec(memory_space=pl.ANY)] * 3,
         out_specs=(pl.BlockSpec(memory_space=pltpu.VMEM),) * 3,
         scratch_shapes=[
-            vm((Z, Q, W, D), BF16),
+            vm((Z, nt, D), BF16),
             vm((Z, EXTRA, W), BF16),
             vm((G, ns, D), BF16),
             vm((1, nt), F32),
             vm((G * ns, 2 * D), BF16),
             vm((2 * D, Z * nt), BF16),
             vm((Z * nt, 2 * D), BF16),
-            vm((2 * ns, nt), F32),
-            vm((2 * ns, nt), F32),
+            vm((64, nt), F32),
+            vm((64, nt), F32),
             vm((G * ns, 2 * W), F32),
             vm((G * ns, 2 * W), F32),
+            vm((8, 2 * W), F32),
+            vm((8, 2 * W), F32),
             vm((G * ns, 128), F32),
             vm((G * ns, 128), F32),
             vm((G, G, ns), F32),
@@ -389,6 +432,18 @@
             collective_id=0, has_side_effects=True, vmem_limit_bytes=VMEM),
         cost_estimate=pl.CostEstimate(flops=6 * 10**9, bytes_accessed=10**6, transcendentals=10**7),
     )(source, target, potential.reshape(1, nt))
+    f, g, mapped = pl.pallas_call(
+        write_out,
+        out_shape=(
+            jax.ShapeDtypeStruct((1, ns), F32),
+            jax.ShapeDtypeStruct((1, nt), F32),
+            jax.ShapeDtypeStruct((ns, D), BF16),
+        ),
+        in_specs=[pl.BlockSpec(memory_space=pl.ANY)] * 3,
+        out_specs=(pl.BlockSpec(memory_space=pl.ANY),) * 3,
+        scratch_shapes=[dma((3,))],
+        compiler_params=pltpu.CompilerParams(vmem_limit_bytes=VMEM),
+    )(f, g, mapped)
     return f.reshape(ns), g.reshape(nt), mapped
 
 

time: 59.8 us -> 58.9 us (0.985)
  local copies, waits for them, and re-layouts: 3.05 us -> 0 us
  Pallas kernels: 55.9 us -> 58.2 us
    unnamed x7 -> x0, local copies, waits for them, and re-layouts: 3.05 us -> none
    pallas_call x0 -> x1, Pallas kernels: none -> 2.2 us  [local(): pl.pallas_call(write_out, out_shape=(jax.ShapeDtypeStruct((1, ns), F32),...]
where the time goes in v2:
time: 58.9 us; the launch traced here: 58.8 us
  Pallas kernels  58.2 us (99%)
  between operations  0.64 us (1%)
    pallas_call x1, Pallas kernels, local(): pl.pallas_call(functools.partial(kernel, dims), out_shape=(jax.ShapeDtype...  56 us
    pallas_call x1, Pallas kernels, local(): pl.pallas_call(write_out, out_shape=(jax.ShapeDtypeStruct((1, ns), F32),...  2.2 us

profile of v2, /device:TPU:1, one launch (start us, length us, event | category | flops | bytes accessed | tf_op | source)
XLA Modules:
  0.0 58.8 jit_solution(15570312150788438078)
XLA Ops:
  0.6 56.0 %shard_map.58 = (f32[1,128]{1,0:T(1,128)}, f32[1,512]{1,0:T(1,128)}, bf16[128,128]{1,0:T(8,128)(2,1)}) custom-call(bf16[128,128]{1,0:T(8,128)(2,1)} %src.1, bf16[512,128]{1,0:T(8,128)(2,1)} %tgt.1, f32[1,512]{1,0:T(1,128)} %bitcast.3), custom_call_target="tpu_custom_call" | custom-call | flops 6000000000 | bytes 1000000 | tf_op jit(solution)/shard_map/pallas_call | solution.py:383
  56.6 2.2 %shard_map.59 = (f32[1,128]{1,0:T(1,128)}, f32[1,512]{1,0:T(1,128)}, bf16[128,128]{1,0:T(8,128)(2,1)}) custom-call(f32[1,128]{1,0:T(1,128)} %get-tuple-element.9.f, f32[1,512]{1,0:T(1,128)} %get-tuple-element.10.g, bf16[128,128]{1,0:T(8,128)(2,1)} %get-tuple-element.11.mapped), custom_call_target="tpu_custom_call" | custom-call | tf_op jit(solution)/shard_map/pallas_call | solution.py:435

commit v3 on v2

--- a/solution.py
+++ b/solution.py
@@ -37,7 +37,7 @@
     return lax.dot_general(ones, both, (((1,), (1,)), ((), ())), preferred_element_type=F32)[0:1, :]
 
 
-def kernel(dims, src, tgt, pot, f_out, g_out, map_out, tbuf, abuf, sbuf, pbuf, lhs, rhs, ta, buf_a, buf_b, col_a, col_b, top_a, top_b, macc, sacc, lrow, lfin,
+def kernel(dims, src, tgt, pot, f_out, g_out, map_out, tbuf, abuf, sbuf, pbuf, lhs, rhs, ta, uall, lbc, col_a, col_b, top_a, top_b, macc, sacc, lrow, lfin,
            mstage, sstage, mcol, lcol, xbuf, zsend, zbuf, wrep, e2, acc, nsend, nrecv, i_sem, a_send, a_recv, t_send, t_recv, s_send, s_recv,
            r_send, r_recv, x_send, x_recv, z_send, z_recv, n_send, n_recv):
     X, Y, Z, C, ns, nt, D, all_s, all_t = dims
@@ -155,19 +155,19 @@
         offsets = abuf[slot].astype(F32)
         for q in range(Q):
             at = q * CH + slot * W
+            cols = slice(slot * nt + q * W, slot * nt + (q + 1) * W)
             piece = tbuf[slot, q * W:(q + 1) * W, :]
-            rhs[0:D, at:at + W] = piece.T
-            rhs[D:D + EXTRA, at:at + W] = jnp.concatenate(
-                [offsets[q + i * Q:q + i * Q + 1, :] for i in range(3)]
-                + [jnp.ones((3, W), F32), jnp.zeros((EXTRA - 6, W), F32)], axis=0).astype(BF16)
+            rhs[0:D, cols] = piece.T
+            rhs[D:D + EXTRA, cols] = jnp.concatenate(
+                [offsets[q + i * Q:q + i * Q + 1, :] for i in range(3)] + [jnp.zeros((EXTRA - 3, W), F32)],
+                axis=0).astype(BF16)
             ta[at:at + W, 0:D] = piece
 
     RC = 64
     per = G * ns // 2 // RC
 
-    def fold(buf, start):
-        rows = pl.ds(start, RC)
-        pieces = [buf[:, q * W:(q + 1) * W] for q in range(Q)]
+    def fold(u, rows):
+        pieces = [u[:, q * W:(q + 1) * W] for q in range(Q)]
         old = macc[rows, :]
         top = functools.reduce(jnp.maximum, pieces, old)
         total = sacc[rows, :] * jnp.exp2((old - top) * SCALE)
@@ -179,14 +179,13 @@
     def row_pass(slot):
         @pl.loop(0, 2)
         def _(p):
-            right_side = jnp.concatenate([rhs[:, q * CH + slot * W:q * CH + (slot + 1) * W] for q in range(Q)], axis=1)
+            cols = slice(slot * nt, (slot + 1) * nt)
             start = pl.multiple_of(p * per * RC, per * RC)
-            bufs = (buf_a, buf_b)
-            for i in range(per + 1):
-                if i < per:
-                    bufs[i % 2][...] = jnp.dot(lhs[pl.ds(start + i * RC, RC), :], right_side, preferred_element_type=F32)
-                if i > 0:
-                    fold(bufs[(i - 1) % 2], start + (i - 1) * RC)
+            for i in range(per):
+                rows = pl.ds(start + i * RC, RC)
+                u = jnp.dot(lhs[rows, :], rhs[:, cols], preferred_element_type=F32)
+                uall[rows, cols] = u
+                fold(u, rows)
 
     waited = {(1, 0), (1, 1), (Z - 1, 0), (Z - 1, 1), (3, 0), (Z - 3, 0), (H, 0)}
 
@@ -222,21 +221,23 @@
     l1 = lse([lrow[i] for i in range(G)])
     lfin[0:G, :] = l1
     for p in range(G):
-        parts = [jnp.zeros((3, ns), F32)] + list(split3(-l1[p:p + 1, :])) + [jnp.zeros((D - 6, ns), F32)]
-        lhs[p * ns:(p + 1) * ns, D:2 * D] = jnp.concatenate(parts, axis=0).T.astype(BF16)
+        lbc[p * ns:(p + 1) * ns, :] = jnp.broadcast_to(l1[p:p + 1, :], (ns, W)).T
     f_out[...] = (0.5 * src_sq - lfin[pl.ds(place, 1), :]) * (1.0 / D) - EPS * math.log(all_s)
 
     MC = 128
     chunks = G * ns // MC
 
-    def scores(buf, tops, at):
-        right_side = rhs[:, pl.ds(pl.multiple_of(at, 2 * W), 2 * W)]
+    def scores(buf, tops, q, slot):
+        cols = [pl.ds(pl.multiple_of((slot + i) * nt + q * W, W), W) for i in range(2)]
         top = None
         for i in range(chunks):
-            u = jnp.dot(lhs[i * MC:(i + 1) * MC, :], right_side, preferred_element_type=F32)
-            buf[i * MC:(i + 1) * MC, :] = u
-            part = jnp.max(u.reshape(MC // 8, 8, 2 * W), axis=0)
-            top = part if top is None else jnp.maximum(top, part)
+            for j in range(0, MC, 32):
+                rows = slice(i * MC + j, i * MC + j + 32)
+                less = lbc[rows, :]
+                u = jnp.concatenate([uall[rows, col] - less for col in cols], axis=1)
+                buf[rows, :] = u
+                part = jnp.max(u.reshape(4, 8, 2 * W), axis=0)
+                top = part if top is None else jnp.maximum(top, part)
             yield
         tops[...] = jnp.broadcast_to(jnp.max(top, axis=0, keepdims=True), (8, 2 * W))
         yield
@@ -268,9 +269,10 @@
         def _(t):
             slot = t * 4
             at = q * CH + slot * W
-            together(scores(col_b, top_b, at + 2 * W), column(col_a, top_a, slot, at))
-            after = at + 4 * W if q < Q - 1 else jnp.minimum(at + 4 * W, Z * nt - 2 * W)
-            together(scores(col_a, top_a, after), column(col_b, top_b, slot + 2, at + 2 * W))
+            together(scores(col_b, top_b, q, slot + 2), column(col_a, top_a, slot, at))
+            ahead = jnp.where(t < Z // 4 - 1, slot + 4, 0)
+            together(scores(col_a, top_a, jnp.minimum(q + (t + 1) // (Z // 4), Q - 1), ahead),
+                     column(col_b, top_b, slot + 2, at + 2 * W))
 
         mcol[q] = jnp.concatenate([mstage[r, 0:1, :] for r in range(Z)], axis=0)
         total = jnp.concatenate([sstage[r, 0:1, :] for r in range(Z)], axis=0)
@@ -294,7 +296,8 @@
             got = zbuf[q * (Z - 1) + d - 1]
             terms.append(jnp.concatenate([got[d:Z, :], got[0:d, :]], axis=0))
         l2 = lse(terms)
-        g_out[0:1, q * W:(q + 1) * W] = (0.5 * own_sq[q] - l2[0:1, :]) * (1.0 / D) + EPS * (math.log(all_s) - math.log(all_t))
+        g_out[0:1, q * W:(q + 1) * W] = pbuf[0:1, q * W:(q + 1) * W] - l2[0:1, :] * (1.0 / D) + EPS * (
+            math.log(all_s) - math.log(all_t))
         w = jnp.exp2((mcol[q] - l2) * SCALE)
         for r in range(Z):
             wrep[q, :, r * W:(r + 1) * W] = jnp.broadcast_to(w[r:r + 1, :], (16, W)).astype(BF16)
@@ -320,7 +323,7 @@
         def _(t):
             weighted(q, pl.multiple_of(t * pair, pair), q == 0)
 
-    together(scores(col_a, top_a, 0))
+    together(scores(col_a, top_a, 0, 0))
     for q in range(Q):
         column_chunk(q)
         if q > 0:
@@ -397,8 +400,8 @@
             vm((G * ns, 2 * D), BF16),
             vm((2 * D, Z * nt), BF16),
             vm((Z * nt, 2 * D), BF16),
-            vm((64, nt), F32),
-            vm((64, nt), F32),
+            vm((G * ns, Z * nt), F32),
+            vm((G * ns, W), F32),
             vm((G * ns, 2 * W), F32),
             vm((G * ns, 2 * W), F32),
             vm((8, 2 * W), F32),

time: 58.9 us -> 57.3 us (0.973)
  Pallas kernels: 58.2 us -> 56.6 us
    pallas_call x1, Pallas kernels: 56 us -> 54.4 us  [local(): pl.pallas_call(functools.partial(kernel, dims), out_shape=(jax.ShapeDtype...]
where the time goes in v3:
time: 57.3 us; the launch traced here: 57.2 us
  Pallas kernels  56.6 us (99%)
  between operations  0.64 us (1%)
    pallas_call x1, Pallas kernels, local(): pl.pallas_call(functools.partial(kernel, dims), out_shape=(jax.ShapeDtype...  54.4 us
    pallas_call x1, Pallas kernels, local(): pl.pallas_call(write_out, out_shape=(jax.ShapeDtypeStruct((1, ns), F32),...  2.2 us

profile of v3, /device:TPU:1, one launch (start us, length us, event | category | flops | bytes accessed | tf_op | source)
XLA Modules:
  0.0 57.2 jit_solution(4470545053698284615)
XLA Ops:
  0.6 54.4 %shard_map.58 = (f32[1,128]{1,0:T(1,128)}, f32[1,512]{1,0:T(1,128)}, bf16[128,128]{1,0:T(8,128)(2,1)}) custom-call(bf16[128,128]{1,0:T(8,128)(2,1)} %src.1, bf16[512,128]{1,0:T(8,128)(2,1)} %tgt.1, f32[1,512]{1,0:T(1,128)} %bitcast.3), custom_call_target="tpu_custom_call" | custom-call | flops 6000000000 | bytes 1000000 | tf_op jit(solution)/shard_map/pallas_call | solution.py:386
  55.0 2.2 %shard_map.59 = (f32[1,128]{1,0:T(1,128)}, f32[1,512]{1,0:T(1,128)}, bf16[128,128]{1,0:T(8,128)(2,1)}) custom-call(f32[1,128]{1,0:T(1,128)} %get-tuple-element.9.f, f32[1,512]{1,0:T(1,128)} %get-tuple-element.10.g, bf16[128,128]{1,0:T(8,128)(2,1)} %get-tuple-element.11.mapped), custom_call_target="tpu_custom_call" | custom-call | tf_op jit(solution)/shard_map/pallas_call | solution.py:438

commit v4 on v3

--- a/solution.py
+++ b/solution.py
@@ -38,7 +38,7 @@
 
 
 def kernel(dims, src, tgt, pot, f_out, g_out, map_out, tbuf, abuf, sbuf, pbuf, lhs, rhs, ta, uall, lbc, col_a, col_b, top_a, top_b, macc, sacc, lrow, lfin,
-           mstage, sstage, mcol, lcol, xbuf, zsend, zbuf, wrep, e2, acc, nsend, nrecv, i_sem, a_send, a_recv, t_send, t_recv, s_send, s_recv,
+           mstage, sstage, mcol, lcol, xbuf, zsend, zbuf, wrep, e2, acc, plan, nsend, nrecv, i_sem, a_send, a_recv, t_send, t_recv, s_send, s_recv,
            r_send, r_recv, x_send, x_recv, z_send, z_recv, n_send, n_recv):
     X, Y, Z, C, ns, nt, D, all_s, all_t = dims
     G = Y * C
@@ -164,10 +164,10 @@
             ta[at:at + W, 0:D] = piece
 
     RC = 64
-    per = G * ns // 2 // RC
-
-    def fold(u, rows):
-        pieces = [u[:, q * W:(q + 1) * W] for q in range(Q)]
+    RM = 2 * ns
+
+    def fold(rows, cols):
+        pieces = [uall[rows, cols + q * W:cols + (q + 1) * W] for q in range(Q)]
         old = macc[rows, :]
         top = functools.reduce(jnp.maximum, pieces, old)
         total = sacc[rows, :] * jnp.exp2((old - top) * SCALE)
@@ -177,15 +177,13 @@
         sacc[rows, :] = total
 
     def row_pass(slot):
-        @pl.loop(0, 2)
-        def _(p):
-            cols = slice(slot * nt, (slot + 1) * nt)
-            start = pl.multiple_of(p * per * RC, per * RC)
-            for i in range(per):
-                rows = pl.ds(start + i * RC, RC)
-                u = jnp.dot(lhs[rows, :], rhs[:, cols], preferred_element_type=F32)
-                uall[rows, cols] = u
-                fold(u, rows)
+        at = slot * nt
+        for i in range(0, G * ns + RM, RM):
+            if i < G * ns:
+                uall[i:i + RM, at:at + nt] = jnp.dot(lhs[i:i + RM, :], rhs[:, at:at + nt], preferred_element_type=F32)
+            if i > 0:
+                for j in range(i - RM, i, RC):
+                    fold(slice(j, j + RC), at)
 
     waited = {(1, 0), (1, 1), (Z - 1, 0), (Z - 1, 1), (3, 0), (Z - 3, 0), (H, 0)}
 
@@ -304,24 +302,20 @@
 
     pair = C * ns
 
-    KC = CH // 2
-
-    def weighted(q, start, first):
-        for i in range(0, pair, MC):
-            rows = pl.ds(start + i, MC)
-            total = None if first else acc[rows, :]
-            for k in range(0, CH, KC):
-                plan = e2[rows, q * CH + k:q * CH + k + KC].reshape(MC // 16, 16, KC) * wrep[q, :, k:k + KC][None]
-                got = jnp.dot(plan.reshape(MC, KC), ta[q * CH + k:q * CH + k + KC, :], preferred_element_type=F32)
-                total = got if total is None else total + got
-            acc[rows, :] = total
+    def weigh(q, rows):
+        for i in range(0, rows.size, 64):
+            part = pl.ds(rows.start + i, 64)
+            plan[part, :] = (e2[part, q * CH:(q + 1) * CH].reshape(4, 16, CH) * wrep[q][None]).reshape(64, CH)
+
+    def weighted(q, rows):
+        got = jnp.dot(plan[rows, :], ta[q * CH:(q + 1) * CH, :], preferred_element_type=F32)
+        acc[rows, :] = got if q == 0 else acc[rows, :] + got
 
     def add_chunk(q):
         weights(q)
-
-        @pl.loop(0, Y)
-        def _(t):
-            weighted(q, pl.multiple_of(t * pair, pair), q == 0)
+        weigh(q, pl.ds(0, G * ns))
+        for i in range(2):
+            weighted(q, pl.ds(i * (G * ns // 2), G * ns // 2))
 
     together(scores(col_a, top_a, 0, 0))
     for q in range(Q):
@@ -339,7 +333,9 @@
     own = None
     for dy in sorted(range(1, Y), key=lambda d: -min(d, Y - d)) + [0]:
         start = pl.multiple_of(((y + dy) % Y) * pair, pair)
-        weighted(Q - 1, start, False)
+        rows = pl.ds(start, pair)
+        weigh(Q - 1, rows)
+        weighted(Q - 1, rows)
         for dc in reversed(range(C)):
             rows = pl.ds(pl.multiple_of(start + ((c + dc) % C) * ns, ns), ns)
             num, den = acc[rows, 0:D], acc[rows, D:2 * D]
@@ -420,6 +416,7 @@
             vm((Q, 16, Z * W), BF16),
             vm((G * ns, Z * nt), BF16),
             vm((G * ns, 2 * D), F32),
+            vm((G * ns, Z * W), BF16),
             vm((G - 1, ns + 16, D), BF16),
             vm((G - 1, ns + 16, D), BF16),
             dma((Q + 2,)),

time: 57.3 us -> 54.1 us (0.944)
  Pallas kernels: 56.6 us -> 53.2 us
    pallas_call x1, Pallas kernels: 54.4 us -> 51 us  [local(): pl.pallas_call(functools.partial(kernel, dims), out_shape=(jax.ShapeDtype...]
where the time goes in v4:
time: 54.1 us; the launch traced here: 54 us
  Pallas kernels  53.2 us (98%)
  between operations  0.8 us (1%)
    pallas_call x1, Pallas kernels, local(): pl.pallas_call(functools.partial(kernel, dims), out_shape=(jax.ShapeDtype...  51 us
    pallas_call x1, Pallas kernels, local(): pl.pallas_call(write_out, out_shape=(jax.ShapeDtypeStruct((1, ns), F32),...  2.2 us

profile of v4, /device:TPU:1, one launch (start us, length us, event | category | flops | bytes accessed | tf_op | source)
XLA Modules:
  0.0 54.0 jit_solution(11758710166894694392)
XLA Ops:
  0.6 51.0 %shard_map.58 = (f32[1,128]{1,0:T(1,128)}, f32[1,512]{1,0:T(1,128)}, bf16[128,128]{1,0:T(8,128)(2,1)}) custom-call(bf16[128,128]{1,0:T(8,128)(2,1)} %src.1, bf16[512,128]{1,0:T(8,128)(2,1)} %tgt.1, f32[1,512]{1,0:T(1,128)} %bitcast.3), custom_call_target="tpu_custom_call" | custom-call | flops 6000000000 | bytes 1000000 | tf_op jit(solution)/shard_map/pallas_call | solution.py:382
  51.7 2.2 %shard_map.59 = (f32[1,128]{1,0:T(1,128)}, f32[1,512]{1,0:T(1,128)}, bf16[128,128]{1,0:T(8,128)(2,1)}) custom-call(f32[1,128]{1,0:T(1,128)} %get-tuple-element.9.f, f32[1,512]{1,0:T(1,128)} %get-tuple-element.10.g, bf16[128,128]{1,0:T(8,128)(2,1)} %get-tuple-element.11.mapped), custom_call_target="tpu_custom_call" | custom-call | tf_op jit(solution)/shard_map/pallas_call | solution.py:435

commit v5 on v4

--- a/solution.py
+++ b/solution.py
@@ -226,7 +226,7 @@
     chunks = G * ns // MC
 
     def scores(buf, tops, q, slot):
-        cols = [pl.ds(pl.multiple_of((slot + i) * nt + q * W, W), W) for i in range(2)]
+        cols = [slice((slot + i) * nt + q * W, (slot + i) * nt + (q + 1) * W) for i in range(2)]
         top = None
         for i in range(chunks):
             for j in range(0, MC, 32):
@@ -248,7 +248,7 @@
                 rows = slice(i * MC + j, i * MC + j + 32)
                 e = jnp.exp2((buf[rows, :].reshape(4, 8, 2 * W) - top[None]) * SCALE)
                 total = total + jnp.sum(e, axis=0)
-                e2[rows, pl.ds(pl.multiple_of(at, 2 * W), 2 * W)] = e.reshape(32, 2 * W).astype(BF16)
+                e2[rows, at:at + 2 * W] = e.reshape(32, 2 * W).astype(BF16)
             yield
         total = jnp.broadcast_to(jnp.sum(total, axis=0, keepdims=True), (8, 2 * W))
         for i in range(2):
@@ -262,15 +262,16 @@
 
     x_copies, z_copies = {}, {}
 
+    tiles = [(q, slot) for q in range(Q) for slot in range(0, Z, 2)]
+
     def column_chunk(q):
-        @pl.loop(0, Z // 4)
-        def _(t):
-            slot = t * 4
-            at = q * CH + slot * W
-            together(scores(col_b, top_b, q, slot + 2), column(col_a, top_a, slot, at))
-            ahead = jnp.where(t < Z // 4 - 1, slot + 4, 0)
-            together(scores(col_a, top_a, jnp.minimum(q + (t + 1) // (Z // 4), Q - 1), ahead),
-                     column(col_b, top_b, slot + 2, at + 2 * W))
+        for n, (tile_q, slot) in enumerate(tiles):
+            if tile_q == q:
+                here, there = ((col_a, top_a), (col_b, top_b)) if n % 2 == 0 else ((col_b, top_b), (col_a, top_a))
+                steps = [column(*here, slot, q * CH + slot * W)]
+                if n + 1 < len(tiles):
+                    steps.insert(0, scores(*there, *tiles[n + 1]))
+                together(*steps)
 
         mcol[q] = jnp.concatenate([mstage[r, 0:1, :] for r in range(Z)], axis=0)
         total = jnp.concatenate([sstage[r, 0:1, :] for r in range(Z)], axis=0)
@@ -320,11 +321,9 @@
     together(scores(col_a, top_a, 0, 0))
     for q in range(Q):
         column_chunk(q)
-        if q > 0:
-            across_z(q - 1)
-    add_chunk(0)
-    across_z(Q - 1)
-    for q in range(1, Q - 1):
+    for q in range(Q):
+        across_z(q)
+    for q in range(Q - 1):
         add_chunk(q)
     weights(Q - 1)
 

time: 54.1 us -> 51.5 us (0.952)
  Pallas kernels: 53.2 us -> 50.8 us
    pallas_call x1, Pallas kernels: 51 us -> 48.6 us  [local(): pl.pallas_call(functools.partial(kernel, dims), out_shape=(jax.ShapeDtype...]
where the time goes in v5:
time: 51.5 us; the launch traced here: 51.4 us
  Pallas kernels  50.8 us (99%)
  between operations  0.64 us (1%)
    pallas_call x1, Pallas kernels, local(): pl.pallas_call(functools.partial(kernel, dims), out_shape=(jax.ShapeDtype...  48.6 us
    pallas_call x1, Pallas kernels, local(): pl.pallas_call(write_out, out_shape=(jax.ShapeDtypeStruct((1, ns), F32),...  2.2 us

profile of v5, /device:TPU:1, one launch (start us, length us, event | category | flops | bytes accessed | tf_op | source)
XLA Modules:
  0.0 51.4 jit_solution(10641151817451041011)
XLA Ops:
  0.6 48.6 %shard_map.58 = (f32[1,128]{1,0:T(1,128)}, f32[1,512]{1,0:T(1,128)}, bf16[128,128]{1,0:T(8,128)(2,1)}) custom-call(bf16[128,128]{1,0:T(8,128)(2,1)} %src.1, bf16[512,128]{1,0:T(8,128)(2,1)} %tgt.1, f32[1,512]{1,0:T(1,128)} %bitcast.3), custom_call_target="tpu_custom_call" | custom-call | flops 6000000000 | bytes 1000000 | tf_op jit(solution)/shard_map/pallas_call | solution.py:381
  49.2 2.2 %shard_map.59 = (f32[1,128]{1,0:T(1,128)}, f32[1,512]{1,0:T(1,128)}, bf16[128,128]{1,0:T(8,128)(2,1)}) custom-call(f32[1,128]{1,0:T(1,128)} %get-tuple-element.9.f, f32[1,512]{1,0:T(1,128)} %get-tuple-element.10.g, bf16[128,128]{1,0:T(8,128)(2,1)} %get-tuple-element.11.mapped), custom_call_target="tpu_custom_call" | custom-call | tf_op jit(solution)/shard_map/pallas_call | solution.py:434

commit v6 on v5

--- a/solution.py
+++ b/solution.py
@@ -92,6 +92,8 @@
         lhs[p * ns:(p + 1) * ns, D:2 * D] = jnp.where(lanes < 3, 1.0, 0.0).astype(BF16)
     pl.semaphore_wait(barrier, len(peers))
 
+    s_copies = [remote(src, sbuf.at[place], s_send.at[i], s_recv.at[i], group_dev(*g)) for i, g in enumerate(group)]
+
     H = Z // 2
     half = nt // 2
     t_copies = {}
@@ -131,8 +133,6 @@
             k = r * Q + d
             t_copies[r, d] = remote(
                 tbuf.at[r, own_piece, :], tbuf.at[r, own_piece, :], t_send.at[k], t_recv.at[k], dev((x + d) % X, y, z, c))
-
-    s_copies = [remote(src, sbuf.at[place], s_send.at[i], s_recv.at[i], group_dev(*g)) for i, g in enumerate(group)]
 
     for cp in fetch:
         cp.wait()
@@ -164,7 +164,7 @@
             ta[at:at + W, 0:D] = piece
 
     RC = 64
-    RM = 2 * ns
+    RM = 4 * ns
 
     def fold(rows, cols):
         pieces = [uall[rows, cols + q * W:cols + (q + 1) * W] for q in range(Q)]
@@ -187,13 +187,16 @@
 
     waited = {(1, 0), (1, 1), (Z - 1, 0), (Z - 1, 1), (3, 0), (Z - 3, 0), (H, 0)}
 
-    def arrive(slot):
-        a_copies[slot - 1].wait_recv()
-        for (r, k), cp in t_copies.items():
-            if r == slot and (r, k) not in waited:
-                cp.wait_recv()
-        take(slot)
-        row_pass(slot)
+    def arrive(*slots):
+        for slot in slots:
+            a_copies[slot - 1].wait_recv()
+            for (r, k), cp in t_copies.items():
+                if r == slot and (r, k) not in waited:
+                    cp.wait_recv()
+        for slot in slots:
+            take(slot)
+        for slot in slots:
+            row_pass(slot)
 
     take(0)
     pass_on(1, 0)
@@ -202,14 +205,16 @@
     spread(H)
     pass_on(1, 1)
     pass_on(Z - 1, 1)
-    for slot in (1, Z - 1, 3, Z - 3, 2, Z - 2, H):
-        arrive(slot)
+    arrive(1, Z - 1)
+    arrive(3, Z - 3)
+    arrive(2, Z - 2)
+    arrive(H)
 
     for p in range(G):
-        m = macc[p * ns:(p + 1) * ns, :].T
-        s = sacc[p * ns:(p + 1) * ns, :].T
-        top = jnp.max(m, axis=0, keepdims=True)
-        total = jnp.sum(s * jnp.exp2((m - top) * SCALE), axis=0, keepdims=True)
+        rows = slice(p * ns, (p + 1) * ns)
+        part = (macc[rows, :] + jnp.log2(sacc[rows, :]) * (1.0 / SCALE)).T
+        top = jnp.max(part, axis=0, keepdims=True)
+        total = jnp.sum(jnp.exp2((part - top) * SCALE), axis=0, keepdims=True)
         lrow[0, p:p + 1, :] = top + jnp.log2(total) * (1.0 / SCALE)
     r_copies = [
         remote(lrow.at[0], lrow.at[i + 1], r_send.at[i], r_recv.at[i], group_dev(*g)) for i, g in enumerate(group)]
@@ -363,12 +368,16 @@
         cp.wait_send()
 
 
-def write_out(f, g, mapped, f_out, g_out, map_out, sem):
-    copies = [
-        pltpu.make_async_copy(a, b, sem.at[i]) for i, (a, b) in enumerate(((f, f_out), (g, g_out), (mapped, map_out)))]
-    for cp in copies:
+def write_out(f, g, mapped, f_out, g_out, map_out, f_mid, g_mid, map_mid, sem):
+    arrays = ((f, f_mid, f_out), (g, g_mid, g_out), (mapped, map_mid, map_out))
+    into = [pltpu.make_async_copy(a, b, sem.at[i]) for i, (a, b, _) in enumerate(arrays)]
+    out = [pltpu.make_async_copy(b, c, sem.at[3 + i]) for i, (_, b, c) in enumerate(arrays)]
+    for cp in into:
         cp.start()
-    for cp in copies:
+    for i in (2, 1, 0):
+        into[i].wait()
+        out[i].start()
+    for cp in out:
         cp.wait()
 
 
@@ -440,7 +449,7 @@
         ),
         in_specs=[pl.BlockSpec(memory_space=pl.ANY)] * 3,
         out_specs=(pl.BlockSpec(memory_space=pl.ANY),) * 3,
-        scratch_shapes=[dma((3,))],
+        scratch_shapes=[vm((1, ns), F32), vm((1, nt), F32), vm((ns, D), BF16), dma((6,))],
         compiler_params=pltpu.CompilerParams(vmem_limit_bytes=VMEM),
     )(f, g, mapped)
     return f.reshape(ns), g.reshape(nt), mapped

time: 51.5 us -> 50.6 us (0.983)
  Pallas kernels: 50.8 us -> 49.8 us
    pallas_call x1, Pallas kernels: 2.2 us -> 1.43 us  [local(): pl.pallas_call(write_out, out_shape=(jax.ShapeDtypeStruct((1, ns), F32),...]
where the time goes in v6:
time: 50.6 us; the launch traced here: 50.5 us
  Pallas kernels  49.8 us (98%)
  between operations  0.64 us (1%)
    pallas_call x1, Pallas kernels, local(): pl.pallas_call(functools.partial(kernel, dims), out_shape=(jax.ShapeDtype...  48.4 us
    pallas_call x1, Pallas kernels, local(): pl.pallas_call(write_out, out_shape=(jax.ShapeDtypeStruct((1, ns), F32),...  1.43 us

profile of v6, /device:TPU:1, one launch (start us, length us, event | category | flops | bytes accessed | tf_op | source)
XLA Modules:
  0.0 50.5 jit_solution(10405017453353685195)
XLA Ops:
  0.6 48.4 %shard_map.58 = (f32[1,128]{1,0:T(1,128)}, f32[1,512]{1,0:T(1,128)}, bf16[128,128]{1,0:T(8,128)(2,1)}) custom-call(bf16[128,128]{1,0:T(8,128)(2,1)} %src.1, bf16[512,128]{1,0:T(8,128)(2,1)} %tgt.1, f32[1,512]{1,0:T(1,128)} %bitcast.3), custom_call_target="tpu_custom_call" | custom-call | flops 6000000000 | bytes 1000000 | tf_op jit(solution)/shard_map/pallas_call | solution.py:390
  49.0 1.4 %shard_map.59 = (f32[1,128]{1,0:T(1,128)}, f32[1,512]{1,0:T(1,128)}, bf16[128,128]{1,0:T(8,128)(2,1)}) custom-call(f32[1,128]{1,0:T(1,128)} %get-tuple-element.9.f, f32[1,512]{1,0:T(1,128)} %get-tuple-element.10.g, bf16[128,128]{1,0:T(8,128)(2,1)} %get-tuple-element.11.mapped), custom_call_target="tpu_custom_call" | custom-call | tf_op jit(solution)/shard_map/pallas_call | solution.py:443

commit v7 on v6

--- a/solution.py
+++ b/solution.py
@@ -31,13 +31,17 @@
     return hi, mid, x - hi - mid
 
 
+def nt_dot(a, b):
+    return lax.dot_general(a, b, (((1,), (1,)), ((), ())), preferred_element_type=F32)
+
+
 def squares(rows):
     both = jnp.concatenate(split2(jnp.square(rows.astype(F32))), axis=1)
     ones = jnp.ones((8, both.shape[1]), BF16)
-    return lax.dot_general(ones, both, (((1,), (1,)), ((), ())), preferred_element_type=F32)[0:1, :]
-
-
-def kernel(dims, src, tgt, pot, f_out, g_out, map_out, tbuf, abuf, sbuf, pbuf, lhs, rhs, ta, uall, lbc, col_a, col_b, top_a, top_b, macc, sacc, lrow, lfin,
+    return nt_dot(ones, both)[0:1, :]
+
+
+def kernel(dims, src, tgt, pot, f_out, g_out, map_out, tbuf, abuf, sbuf, pbuf, ta, uall, lbc, col_a, col_b, top_a, top_b, macc, sacc, lrow, lfin,
            mstage, sstage, mcol, lcol, xbuf, zsend, zbuf, wrep, e2, acc, plan, nsend, nrecv, i_sem, a_send, a_recv, t_send, t_recv, s_send, s_recv,
            r_send, r_recv, x_send, x_recv, z_send, z_recv, n_send, n_recv):
     X, Y, Z, C, ns, nt, D, all_s, all_t = dims
@@ -83,13 +87,9 @@
     fetch.append(pltpu.make_async_copy(src, sbuf.at[place], i_sem.at[Q + 1]))
     for cp in fetch:
         cp.start()
-    rhs[D + EXTRA:2 * D, :] = jnp.zeros((D - EXTRA, Z * nt), BF16)
     macc[...] = jnp.full(macc.shape, LOW, F32)
     sacc[...] = jnp.zeros(sacc.shape, F32)
     ta[:, D:2 * D] = jnp.ones((Z * nt, D), BF16)
-    lanes = lax.broadcasted_iota(jnp.int32, (ns, D), 1)
-    for p in range(G):
-        lhs[p * ns:(p + 1) * ns, D:2 * D] = jnp.where(lanes < 3, 1.0, 0.0).astype(BF16)
     pl.semaphore_wait(barrier, len(peers))
 
     s_copies = [remote(src, sbuf.at[place], s_send.at[i], s_recv.at[i], group_dev(*g)) for i, g in enumerate(group)]
@@ -148,26 +148,19 @@
 
     for cp in s_copies:
         cp.wait_recv()
-    for p in range(G):
-        lhs[p * ns:(p + 1) * ns, 0:D] = sbuf[p]
 
     def take(slot):
-        offsets = abuf[slot].astype(F32)
         for q in range(Q):
             at = q * CH + slot * W
-            cols = slice(slot * nt + q * W, slot * nt + (q + 1) * W)
-            piece = tbuf[slot, q * W:(q + 1) * W, :]
-            rhs[0:D, cols] = piece.T
-            rhs[D:D + EXTRA, cols] = jnp.concatenate(
-                [offsets[q + i * Q:q + i * Q + 1, :] for i in range(3)] + [jnp.zeros((EXTRA - 3, W), F32)],
-                axis=0).astype(BF16)
-            ta[at:at + W, 0:D] = piece
-
-    RC = 64
-    RM = 4 * ns
-
-    def fold(rows, cols):
-        pieces = [uall[rows, cols + q * W:cols + (q + 1) * W] for q in range(Q)]
+            ta[at:at + W, 0:D] = tbuf[slot, q * W:(q + 1) * W, :]
+
+    RC = 32
+    RP = G // 2
+
+    def fold(rows, slots, offsets):
+        pieces = [
+            uall[rows, slot * nt + q * W:slot * nt + (q + 1) * W] + offset[q:q + 1, :]
+            for slot, offset in zip(slots, offsets) for q in range(Q)]
         old = macc[rows, :]
         top = functools.reduce(jnp.maximum, pieces, old)
         total = sacc[rows, :] * jnp.exp2((old - top) * SCALE)
@@ -176,14 +169,19 @@
         macc[rows, :] = top
         sacc[rows, :] = total
 
-    def row_pass(slot):
-        at = slot * nt
-        for i in range(0, G * ns + RM, RM):
-            if i < G * ns:
-                uall[i:i + RM, at:at + nt] = jnp.dot(lhs[i:i + RM, :], rhs[:, at:at + nt], preferred_element_type=F32)
-            if i > 0:
-                for j in range(i - RM, i, RC):
-                    fold(slice(j, j + RC), at)
+    def row_pass(*slots):
+        offsets = []
+        for slot in slots:
+            parts = abuf[slot].astype(F32)
+            offsets.append(parts[0:Q, :] + parts[Q:2 * Q, :] + parts[2 * Q:3 * Q, :])
+        for p in range(0, G + RP, RP):
+            if p < G:
+                for slot in slots:
+                    uall[p * ns:(p + RP) * ns, slot * nt:(slot + 1) * nt] = nt_dot(
+                        sbuf[p:p + RP].reshape(RP * ns, D), tbuf[slot])
+            if p > 0:
+                for j in range((p - RP) * ns, p * ns, RC):
+                    fold(slice(j, j + RC), slots, offsets)
 
     waited = {(1, 0), (1, 1), (Z - 1, 0), (Z - 1, 1), (3, 0), (Z - 3, 0), (H, 0)}
 
@@ -195,8 +193,7 @@
                     cp.wait_recv()
         for slot in slots:
             take(slot)
-        for slot in slots:
-            row_pass(slot)
+        row_pass(*slots)
 
     take(0)
     pass_on(1, 0)
@@ -300,8 +297,7 @@
             got = zbuf[q * (Z - 1) + d - 1]
             terms.append(jnp.concatenate([got[d:Z, :], got[0:d, :]], axis=0))
         l2 = lse(terms)
-        g_out[0:1, q * W:(q + 1) * W] = pbuf[0:1, q * W:(q + 1) * W] - l2[0:1, :] * (1.0 / D) + EPS * (
-            math.log(all_s) - math.log(all_t))
+        g_out[0:1, q * W:(q + 1) * W] = (0.5 * own_sq[q] - l2[0:1, :]) * (1.0 / D) + EPS * (math.log(all_s) - math.log(all_t))
         w = jnp.exp2((mcol[q] - l2) * SCALE)
         for r in range(Z):
             wrep[q, :, r * W:(r + 1) * W] = jnp.broadcast_to(w[r:r + 1, :], (16, W)).astype(BF16)
@@ -401,8 +397,6 @@
             vm((Z, EXTRA, W), BF16),
             vm((G, ns, D), BF16),
             vm((1, nt), F32),
-            vm((G * ns, 2 * D), BF16),
-            vm((2 * D, Z * nt), BF16),
             vm((Z * nt, 2 * D), BF16),
             vm((G * ns, Z * nt), F32),
             vm((G * ns, W), F32),

time: 50.6 us -> 50.8 us (level)
  no operation moved by 1% of the time
where the time goes in v7:
time: 50.8 us; the launch traced here: 50.6 us
  Pallas kernels  50 us (98%)
  between operations  0.64 us (1%)
    pallas_call x1, Pallas kernels, local(): pl.pallas_call(functools.partial(kernel, dims), out_shape=(jax.ShapeDtype...  48.5 us
    pallas_call x1, Pallas kernels, local(): pl.pallas_call(write_out, out_shape=(jax.ShapeDtypeStruct((1, ns), F32),...  1.43 us

profile of v7, /device:TPU:1, one launch (start us, length us, event | category | flops | bytes accessed | tf_op | source)
XLA Modules:
  0.0 50.6 jit_solution(3998124780204908474)
XLA Ops:
  0.6 48.5 %shard_map.58 = (f32[1,128]{1,0:T(1,128)}, f32[1,512]{1,0:T(1,128)}, bf16[128,128]{1,0:T(8,128)(2,1)}) custom-call(bf16[128,128]{1,0:T(8,128)(2,1)} %src.1, bf16[512,128]{1,0:T(8,128)(2,1)} %tgt.1, f32[1,512]{1,0:T(1,128)} %bitcast.3), custom_call_target="tpu_custom_call" | custom-call | flops 6000000000 | bytes 1000000 | tf_op jit(solution)/shard_map/pallas_call | solution.py:386
  49.2 1.4 %shard_map.59 = (f32[1,128]{1,0:T(1,128)}, f32[1,512]{1,0:T(1,128)}, bf16[128,128]{1,0:T(8,128)(2,1)}) custom-call(f32[1,128]{1,0:T(1,128)} %get-tuple-element.9.f, f32[1,512]{1,0:T(1,128)} %get-tuple-element.10.g, bf16[128,128]{1,0:T(8,128)(2,1)} %get-tuple-element.11.mapped), custom_call_target="tpu_custom_call" | custom-call | tf_op jit(solution)/shard_map/pallas_call | solution.py:437

commit v8 on v7

--- a/solution.py
+++ b/solution.py
@@ -16,7 +16,7 @@
 
 Y, Z, C = 4, 8, 2
 LOW = -1e30
-VMEM = 63532032
+VMEM = 48 * 1024 * 1024
 W, EXTRA = 128, 16
 
 
@@ -149,18 +149,11 @@
     for cp in s_copies:
         cp.wait_recv()
 
-    def take(slot):
-        for q in range(Q):
-            at = q * CH + slot * W
-            ta[at:at + W, 0:D] = tbuf[slot, q * W:(q + 1) * W, :]
-
     RC = 32
     RP = G // 2
 
-    def fold(rows, slots, offsets):
-        pieces = [
-            uall[rows, slot * nt + q * W:slot * nt + (q + 1) * W] + offset[q:q + 1, :]
-            for slot, offset in zip(slots, offsets) for q in range(Q)]
+    def fold(rows, pieces):
+        pieces = [uall[rows, slot * nt + q * W:slot * nt + (q + 1) * W] + offset for slot, q, offset in pieces]
         old = macc[rows, :]
         top = functools.reduce(jnp.maximum, pieces, old)
         total = sacc[rows, :] * jnp.exp2((old - top) * SCALE)
@@ -169,43 +162,48 @@
         macc[rows, :] = top
         sacc[rows, :] = total
 
-    def row_pass(*slots):
-        offsets = []
+    def row_pass(slots, first=0, last=Q):
+        pieces = []
         for slot in slots:
             parts = abuf[slot].astype(F32)
-            offsets.append(parts[0:Q, :] + parts[Q:2 * Q, :] + parts[2 * Q:3 * Q, :])
+            offsets = parts[0:Q, :] + parts[Q:2 * Q, :] + parts[2 * Q:3 * Q, :]
+            for q in range(first, last):
+                at = q * CH + slot * W
+                ta[at:at + W, 0:D] = tbuf[slot, q * W:(q + 1) * W, :]
+                pieces.append((slot, q, offsets[q:q + 1, :]))
         for p in range(0, G + RP, RP):
             if p < G:
                 for slot in slots:
-                    uall[p * ns:(p + RP) * ns, slot * nt:(slot + 1) * nt] = nt_dot(
-                        sbuf[p:p + RP].reshape(RP * ns, D), tbuf[slot])
+                    uall[p * ns:(p + RP) * ns, slot * nt + first * W:slot * nt + last * W] = nt_dot(
+                        sbuf[p:p + RP].reshape(RP * ns, D), tbuf[slot, first * W:last * W, :])
             if p > 0:
                 for j in range((p - RP) * ns, p * ns, RC):
-                    fold(slice(j, j + RC), slots, offsets)
-
-    waited = {(1, 0), (1, 1), (Z - 1, 0), (Z - 1, 1), (3, 0), (Z - 3, 0), (H, 0)}
-
-    def arrive(*slots):
-        for slot in slots:
-            a_copies[slot - 1].wait_recv()
-            for (r, k), cp in t_copies.items():
-                if r == slot and (r, k) not in waited:
-                    cp.wait_recv()
-        for slot in slots:
-            take(slot)
-        row_pass(*slots)
-
-    take(0)
+                    fold(slice(j, j + RC), pieces)
+
+    def arrived(slot, k):
+        if (slot, k) in t_copies:
+            t_copies[slot, k].wait_recv()
+
     pass_on(1, 0)
     pass_on(Z - 1, 0)
-    row_pass(0)
+    row_pass([0])
     spread(H)
     pass_on(1, 1)
     pass_on(Z - 1, 1)
-    arrive(1, Z - 1)
-    arrive(3, Z - 3)
-    arrive(2, Z - 2)
-    arrive(H)
+    for cp in a_copies:
+        cp.wait_recv()
+    row_pass([1, Z - 1])
+    for slot in (3, Z - 3):
+        for d in range(1, X):
+            arrived(slot, d)
+    row_pass([3, Z - 3])
+    for h in range(2):
+        arrived(2, h)
+        arrived(Z - 2, h)
+        row_pass([2, Z - 2], h * Q // 2, (h + 1) * Q // 2)
+    for d in range(1, X):
+        arrived(H, d)
+    row_pass([H])
 
     for p in range(G):
         rows = slice(p * ns, (p + 1) * ns)
@@ -364,16 +362,12 @@
         cp.wait_send()
 
 
-def write_out(f, g, mapped, f_out, g_out, map_out, f_mid, g_mid, map_mid, sem):
-    arrays = ((f, f_mid, f_out), (g, g_mid, g_out), (mapped, map_mid, map_out))
-    into = [pltpu.make_async_copy(a, b, sem.at[i]) for i, (a, b, _) in enumerate(arrays)]
-    out = [pltpu.make_async_copy(b, c, sem.at[3 + i]) for i, (_, b, c) in enumerate(arrays)]
-    for cp in into:
+def write_out(f, g, mapped, f_out, g_out, map_out, sem):
+    copies = [
+        pltpu.make_async_copy(a, b, sem.at[i]) for i, (a, b) in enumerate(((mapped, map_out), (g, g_out), (f, f_out)))]
+    for cp in copies:
         cp.start()
-    for i in (2, 1, 0):
-        into[i].wait()
-        out[i].start()
-    for cp in out:
+    for cp in copies:
         cp.wait()
 
 
@@ -433,7 +427,7 @@
         compiler_params=pltpu.CompilerParams(
             collective_id=0, has_side_effects=True, vmem_limit_bytes=VMEM),
         cost_estimate=pl.CostEstimate(flops=6 * 10**9, bytes_accessed=10**6, transcendentals=10**7),
-    )(source, target, potential.reshape(1, nt))
+    )(*[pltpu.with_memory_space_constraint(a, pltpu.HBM) for a in (source, target, potential.reshape(1, nt))])
     f, g, mapped = pl.pallas_call(
         write_out,
         out_shape=(
@@ -441,10 +435,9 @@
             jax.ShapeDtypeStruct((1, nt), F32),
             jax.ShapeDtypeStruct((ns, D), BF16),
         ),
-        in_specs=[pl.BlockSpec(memory_space=pl.ANY)] * 3,
+        in_specs=[pl.BlockSpec(memory_space=pltpu.VMEM)] * 3,
         out_specs=(pl.BlockSpec(memory_space=pl.ANY),) * 3,
-        scratch_shapes=[vm((1, ns), F32), vm((1, nt), F32), vm((ns, D), BF16), dma((6,))],
-        compiler_params=pltpu.CompilerParams(vmem_limit_bytes=VMEM),
+        scratch_shapes=[dma((3,))],
     )(f, g, mapped)
     return f.reshape(ns), g.reshape(nt), mapped
 

time: 50.8 us -> 51.3 us (level)
  local copies, waits for them, and re-layouts: 0 us -> 1.69 us
  Pallas kernels: 50 us -> 48.8 us
    unnamed x0 -> x6, local copies, waits for them, and re-layouts: none -> 1.69 us
    pallas_call x1, Pallas kernels: 48.5 us -> 47.4 us  [local(): pl.pallas_call(functools.partial(kernel, dims), out_shape=(jax.ShapeDtype...]
where the time goes in v8:
time: 51.3 us; the launch traced here: 51.2 us
  Pallas kernels  48.8 us (95%)
  local copies, waits for them, and re-layouts  1.69 us (3%)
  between operations  0.65 us (1%)
    pallas_call x1, Pallas kernels, local(): pl.pallas_call(functools.partial(kernel, dims), out_shape=(jax.ShapeDtype...  47.4 us
    unnamed x6, local copies, waits for them, and re-layouts  1.69 us
    pallas_call x1, Pallas kernels, local(): pl.pallas_call(write_out, out_shape=(jax.ShapeDtypeStruct((1, ns), F32),...  1.41 us

profile of v8, /device:TPU:1, one launch (start us, length us, event | category | flops | bytes accessed | tf_op | source)
XLA Modules:
  0.0 51.2 jit_solution(10762722921491194294)
XLA Ops:
  0.6 47.4 %shard_map.58 = (f32[1,128]{1,0:T(1,128)S(1)}, f32[1,512]{1,0:T(1,128)S(1)}, bf16[128,128]{1,0:T(8,128)(2,1)S(1)}) custom-call(bf16[128,128]{1,0:T(8,128)(2,1)} %src.1, bf16[512,128]{1,0:T(8,128)(2,1)} %tgt.1, f32[1,512]{1,0:T(1,128)} %bitcast.3), custom_call_target="tpu_custom_call" | custom-call | flops 6000000000 | bytes 1000000 | tf_op jit(solution)/shard_map/pallas_call | solution.py:380
  48.1 0.0 copy-start
  48.1 0.6 %copy-done = bf16[128,128]{1,0:T(8,128)(2,1)} copy-done((bf16[128,128]{1,0:T(8,128)(2,1)}, bf16[128,128]{1,0:T(8,128)(2,1)S(1)}, u32[]{:S(2)}) %copy-start) | copy-done | bytes 32792
  48.7 0.0 copy-start.1
  48.7 0.6 %copy-done.1 = f32[1,512]{1,0:T(1,128)} copy-done((f32[1,512]{1,0:T(1,128)}, f32[1,512]{1,0:T(1,128)S(1)}, u32[]{:S(2)}) %copy-start.1) | copy-done | bytes 2072
  49.3 0.0 copy-start.2
  49.3 0.5 copy-done.2
  49.8 1.4 %shard_map.59 = (f32[1,128]{1,0:T(1,128)}, f32[1,512]{1,0:T(1,128)}, bf16[128,128]{1,0:T(8,128)(2,1)}) custom-call(f32[1,128]{1,0:T(1,128)} %copy-done.2, f32[1,512]{1,0:T(1,128)} %copy-done.1, bf16[128,128]{1,0:T(8,128)(2,1)} %copy-done), custom_call_target="tpu_custom_call" | custom-call | tf_op jit(solution)/shard_map/pallas_call | solution.py:431
Async XLA Ops:
  48.1 0.6 %copy-start = (bf16[128,128]{1,0:T(8,128)(2,1)}, bf16[128,128]{1,0:T(8,128)(2,1)S(1)}, u32[]{:S(2)}) copy-start(bf16[128,128]{1,0:T(8,128)(2,1)S(1)} %get-tuple-element.11.mapped) | copy-start | bytes 98308
  48.7 0.6 %copy-start.1 = (f32[1,512]{1,0:T(1,128)}, f32[1,512]{1,0:T(1,128)S(1)}, u32[]{:S(2)}) copy-start(f32[1,512]{1,0:T(1,128)S(1)} %get-tuple-element.10.g) | copy-start | bytes 6148
  49.3 0.5 copy-start.2

commit v9 on v8

--- a/solution.py
+++ b/solution.py
@@ -438,6 +438,7 @@
         in_specs=[pl.BlockSpec(memory_space=pltpu.VMEM)] * 3,
         out_specs=(pl.BlockSpec(memory_space=pl.ANY),) * 3,
         scratch_shapes=[dma((3,))],
+        compiler_params=pltpu.CompilerParams(vmem_limit_bytes=1024 * 1024),
     )(f, g, mapped)
     return f.reshape(ns), g.reshape(nt), mapped
 

time: 51.3 us -> 48.8 us (0.951)
  local copies, waits for them, and re-layouts: 1.69 us -> 0 us
  Pallas kernels: 48.8 us -> 48.1 us
    unnamed x6 -> x0, local copies, waits for them, and re-layouts: 1.69 us -> none
    pallas_call x1, Pallas kernels: 1.41 us -> 0.65 us  [local(): pl.pallas_call(write_out, out_shape=(jax.ShapeDtypeStruct((1, ns), F32),...]
where the time goes in v9:
time: 48.8 us; the launch traced here: 48.7 us
  Pallas kernels  48.1 us (99%)
  between operations  0.64 us (1%)
    pallas_call x1, Pallas kernels, local(): pl.pallas_call(functools.partial(kernel, dims), out_shape=(jax.ShapeDtype...  47.4 us

profile of v9, /device:TPU:1, one launch (start us, length us, event | category | flops | bytes accessed | tf_op | source)
XLA Modules:
  0.0 48.7 jit_solution(4432529559834388076)
XLA Ops:
  0.6 47.4 %shard_map.58 = (f32[1,128]{1,0:T(1,128)S(1)}, f32[1,512]{1,0:T(1,128)S(1)}, bf16[128,128]{1,0:T(8,128)(2,1)S(1)}) custom-call(bf16[128,128]{1,0:T(8,128)(2,1)} %src.1, bf16[512,128]{1,0:T(8,128)(2,1)} %tgt.1, f32[1,512]{1,0:T(1,128)} %bitcast.3), custom_call_target="tpu_custom_call" | custom-call | flops 6000000000 | bytes 1000000 | tf_op jit(solution)/shard_map/pallas_call | solution.py:380
  48.1 0.6 %shard_map.59 = (f32[1,128]{1,0:T(1,128)}, f32[1,512]{1,0:T(1,128)}, bf16[128,128]{1,0:T(8,128)(2,1)}) custom-call(f32[1,128]{1,0:T(1,128)S(1)} %get-tuple-element.9.f, f32[1,512]{1,0:T(1,128)S(1)} %get-tuple-element.10.g, bf16[128,128]{1,0:T(8,128)(2,1)S(1)} %get-tuple-element.11.mapped), custom_call_target="tpu_custom_call" | custom-call | tf_op jit(solution)/shard_map/pallas_call | solution.py:431

commit v10 on v9

--- a/solution.py
+++ b/solution.py
@@ -66,8 +66,8 @@
 
     def lse(items):
         top = functools.reduce(jnp.maximum, items)
-        total = functools.reduce(jnp.add, [jnp.exp2((i - top) * SCALE) for i in items])
-        return top + jnp.log2(total) * (1.0 / SCALE)
+        total = functools.reduce(jnp.add, [jnp.exp2(i - top) for i in items])
+        return top + jnp.log2(total)
 
     group = [(dy, dc) for dy in range(Y) for dc in range(C) if (dy, dc) != (0, 0)]
 
@@ -153,12 +153,17 @@
     RP = G // 2
 
     def fold(rows, pieces):
-        pieces = [uall[rows, slot * nt + q * W:slot * nt + (q + 1) * W] + offset for slot, q, offset in pieces]
+        kept = []
+        for slot, q, offset in pieces:
+            cols = slice(slot * nt + q * W, slot * nt + (q + 1) * W)
+            u = uall[rows, cols] * SCALE
+            uall[rows, cols] = u
+            kept.append(u + offset)
         old = macc[rows, :]
-        top = functools.reduce(jnp.maximum, pieces, old)
-        total = sacc[rows, :] * jnp.exp2((old - top) * SCALE)
-        for piece in pieces:
-            total = total + jnp.exp2((piece - top) * SCALE)
+        top = functools.reduce(jnp.maximum, kept, old)
+        total = sacc[rows, :] * jnp.exp2(old - top)
+        for piece in kept:
+            total = total + jnp.exp2(piece - top)
         macc[rows, :] = top
         sacc[rows, :] = total
 
@@ -166,7 +171,7 @@
         pieces = []
         for slot in slots:
             parts = abuf[slot].astype(F32)
-            offsets = parts[0:Q, :] + parts[Q:2 * Q, :] + parts[2 * Q:3 * Q, :]
+            offsets = (parts[0:Q, :] + parts[Q:2 * Q, :] + parts[2 * Q:3 * Q, :]) * SCALE
             for q in range(first, last):
                 at = q * CH + slot * W
                 ta[at:at + W, 0:D] = tbuf[slot, q * W:(q + 1) * W, :]
@@ -207,10 +212,10 @@
 
     for p in range(G):
         rows = slice(p * ns, (p + 1) * ns)
-        part = (macc[rows, :] + jnp.log2(sacc[rows, :]) * (1.0 / SCALE)).T
+        part = (macc[rows, :] + jnp.log2(sacc[rows, :])).T
         top = jnp.max(part, axis=0, keepdims=True)
-        total = jnp.sum(jnp.exp2((part - top) * SCALE), axis=0, keepdims=True)
-        lrow[0, p:p + 1, :] = top + jnp.log2(total) * (1.0 / SCALE)
+        total = jnp.sum(jnp.exp2(part - top), axis=0, keepdims=True)
+        lrow[0, p:p + 1, :] = top + jnp.log2(total)
     r_copies = [
         remote(lrow.at[0], lrow.at[i + 1], r_send.at[i], r_recv.at[i], group_dev(*g)) for i, g in enumerate(group)]
     src_sq = squares(sbuf[place])
@@ -220,7 +225,7 @@
     lfin[0:G, :] = l1
     for p in range(G):
         lbc[p * ns:(p + 1) * ns, :] = jnp.broadcast_to(l1[p:p + 1, :], (ns, W)).T
-    f_out[...] = (0.5 * src_sq - lfin[pl.ds(place, 1), :]) * (1.0 / D) - EPS * math.log(all_s)
+    f_out[...] = (0.5 * src_sq - lfin[pl.ds(place, 1), :] * (1.0 / SCALE)) * (1.0 / D) - EPS * math.log(all_s)
 
     MC = 128
     chunks = G * ns // MC
@@ -246,7 +251,7 @@
         for i in range(chunks):
             for j in range(0, MC, 32):
                 rows = slice(i * MC + j, i * MC + j + 32)
-                e = jnp.exp2((buf[rows, :].reshape(4, 8, 2 * W) - top[None]) * SCALE)
+                e = jnp.exp2(buf[rows, :].reshape(4, 8, 2 * W) - top[None])
                 total = total + jnp.sum(e, axis=0)
                 e2[rows, at:at + 2 * W] = e.reshape(32, 2 * W).astype(BF16)
             yield
@@ -266,6 +271,8 @@
 
     def column_chunk(q):
         for n, (tile_q, slot) in enumerate(tiles):
+            if n == len(tiles) - 2 and tile_q == q:
+                across_z(0)
             if tile_q == q:
                 here, there = ((col_a, top_a), (col_b, top_b)) if n % 2 == 0 else ((col_b, top_b), (col_a, top_a))
                 steps = [column(*here, slot, q * CH + slot * W)]
@@ -275,7 +282,7 @@
 
         mcol[q] = jnp.concatenate([mstage[r, 0:1, :] for r in range(Z)], axis=0)
         total = jnp.concatenate([sstage[r, 0:1, :] for r in range(Z)], axis=0)
-        lcol[q] = mcol[q] + jnp.log2(total) * (1.0 / SCALE)
+        lcol[q] = mcol[q] + jnp.log2(total)
         for d in range(1, X):
             k = q * (X - 1) + d - 1
             x_copies[q, d] = remote(lcol.at[q], xbuf.at[k], x_send.at[k], x_recv.at[k], dev((x + d) % X, y, z, c))
@@ -295,8 +302,9 @@
             got = zbuf[q * (Z - 1) + d - 1]
             terms.append(jnp.concatenate([got[d:Z, :], got[0:d, :]], axis=0))
         l2 = lse(terms)
-        g_out[0:1, q * W:(q + 1) * W] = (0.5 * own_sq[q] - l2[0:1, :]) * (1.0 / D) + EPS * (math.log(all_s) - math.log(all_t))
-        w = jnp.exp2((mcol[q] - l2) * SCALE)
+        g_out[0:1, q * W:(q + 1) * W] = (0.5 * own_sq[q] - l2[0:1, :] * (1.0 / SCALE)) * (1.0 / D) + EPS * (
+            math.log(all_s) - math.log(all_t))
+        w = jnp.exp2(mcol[q] - l2)
         for r in range(Z):
             wrep[q, :, r * W:(r + 1) * W] = jnp.broadcast_to(w[r:r + 1, :], (16, W)).astype(BF16)
 
@@ -320,7 +328,7 @@
     together(scores(col_a, top_a, 0, 0))
     for q in range(Q):
         column_chunk(q)
-    for q in range(Q):
+    for q in range(1, Q):
         across_z(q)
     for q in range(Q - 1):
         add_chunk(q)

time: 48.8 us -> 49.4 us (1.012)
  Pallas kernels: 48.1 us -> 48.7 us
    pallas_call x1, Pallas kernels: 47.4 us -> 48 us  [local(): pl.pallas_call(functools.partial(kernel, dims), out_shape=(jax.ShapeDtype...]
where the time goes in v10:
time: 49.4 us; the launch traced here: 49.3 us
  Pallas kernels  48.7 us (99%)
  between operations  0.64 us (1%)
    pallas_call x1, Pallas kernels, local(): pl.pallas_call(functools.partial(kernel, dims), out_shape=(jax.ShapeDtype...  48 us

profile of v10, /device:TPU:1, one launch (start us, length us, event | category | flops | bytes accessed | tf_op | source)
XLA Modules:
  0.0 49.3 jit_solution(1974070163142674495)
XLA Ops:
  0.6 48.0 %shard_map.58 = (f32[1,128]{1,0:T(1,128)S(1)}, f32[1,512]{1,0:T(1,128)S(1)}, bf16[128,128]{1,0:T(8,128)(2,1)S(1)}) custom-call(bf16[128,128]{1,0:T(8,128)(2,1)} %src.1, bf16[512,128]{1,0:T(8,128)(2,1)} %tgt.1, f32[1,512]{1,0:T(1,128)} %bitcast.3), custom_call_target="tpu_custom_call" | custom-call | flops 6000000000 | bytes 1000000 | tf_op jit(solution)/shard_map/pallas_call | solution.py:388
  48.7 0.6 %shard_map.59 = (f32[1,128]{1,0:T(1,128)}, f32[1,512]{1,0:T(1,128)}, bf16[128,128]{1,0:T(8,128)(2,1)}) custom-call(f32[1,128]{1,0:T(1,128)S(1)} %get-tuple-element.9.f, f32[1,512]{1,0:T(1,128)S(1)} %get-tuple-element.10.g, bf16[128,128]{1,0:T(8,128)(2,1)S(1)} %get-tuple-element.11.mapped), custom_call_target="tpu_custom_call" | custom-call | tf_op jit(solution)/shard_map/pallas_call | solution.py:439
